TPU v7x, 128 devices: a whole 4x4x4 slice. The times are simulated.
128 devices in a mesh: queue: 32 (over z, y, core), tp: 4 (over x).
Axes of the slice: x: 4, y: 4, z: 4, core: 2. Of those that a mesh axis runs over, the one named last changes fastest.
Arguments:
- latents: bfloat16 [16384, 5120], P('queue'), may hold values from -6 to 6
- noise_level: int32 [64], P('queue'), may hold values from 0 to 31
- lookback: int32 [64], P('queue'), may hold values from 0 to 3, as said below
- level_table: bfloat16 [32, 10240], replicated, may hold values from -3 to 3
- w_query: bfloat16 [5120, 2560], P(None, 'tp'), may hold values from -0.078125 to 0.078125
- w_key: bfloat16 [5120, 2560], P(None, 'tp'), may hold values from -0.078125 to 0.078125
- w_value: bfloat16 [5120, 2560], P(None, 'tp'), may hold values from -0.3125 to 0.3125
- gain_query: float32 [2560], P('tp'), may hold values from 0.5 to 10
- gain_key: float32 [2560], P('tp'), may hold values from 0.5 to 10
Outputs:
- mixed: bfloat16 [16384, 2560], P('queue', 'tp')
Inputs may be any that keep to these rules, and one draw needn't show every extreme that they name: lookback[f] is at most f and at most 3; some frame has exactly 3.
All inputs are finite; a program needn't handle non-finite values.
Results may differ from a plain program's by a relative error of at most 0.015.
The roundings to bfloat16 on the way count: a program that leaves them out, or rounds other values in their place, can miss the bound.
Values may be sent and summed in bfloat16 or wider, within the bound.
No kernel may reach another device: no remote copies, remote signals or barrier semaphores. Data moves between devices by JAX's collectives and lax.ppermute only.
A program may use at most 128 MiB of HBM per device.

v0:
```python
import jax
import jax.numpy as jnp
from jax import lax
from jax.sharding import PartitionSpec as P

HD = 128
WIN = 4


EPSILON = 1e-06


def passed_along(x, axis, by):
    peers = lax.axis_size(axis)
    pairs = [(i, i + by) for i in range(peers) if 0 <= i + by < peers]
    return lax.ppermute(x, axis, pairs)


def level_rows(noise_level, level_table):
    choose = (
        noise_level[:, None]
        == lax.broadcasted_iota(jnp.int32, (noise_level.shape[0], level_table.shape[0]), 1)
    ).astype(jnp.bfloat16)
    return jnp.dot(choose, level_table, preferred_element_type=jnp.float32)


def modulate(latents, modulation, frame_count, frame_rows, model_width):
    shaped = latents.astype(jnp.float32).reshape(frame_count, frame_rows, model_width)
    center = jnp.mean(shaped, axis=2, keepdims=True)
    spread = jnp.mean(jnp.square(shaped - center), axis=2, keepdims=True)
    normed = (shaped - center) * lax.rsqrt(spread + EPSILON)
    shifts = modulation[:, None, :model_width]
    scales = modulation[:, None, model_width:]
    result = normed * (1.0 + scales) + shifts
    return result.reshape(frame_count * frame_rows, model_width).astype(jnp.bfloat16)


def fetch_behind(rows_block, frame_count, frame_rows):
    gathered = []
    remaining = WIN - 1
    moving = rows_block
    distance = 1
    while remaining > 0:
        taken = min(frame_count, remaining)
        outgoing = moving[moving.shape[0] - taken * frame_rows :]
        moving = passed_along(outgoing, "queue", 1)
        gathered.insert(0, moving)
        remaining = remaining - taken
        distance = distance + 1
    return jnp.concatenate(gathered, 0)


def window_attend(queries, keys_win, values_win, reach):
    frame_rows = queries.shape[0]
    head_count = queries.shape[1] // HD
    queries_h = queries.reshape(frame_rows, head_count, HD)
    keys_h = keys_win.reshape(keys_win.shape[0], head_count, HD)
    values_h = values_win.reshape(values_win.shape[0], head_count, HD)
    scores = jnp.einsum(
        "qhd,khd->hqk", queries_h, keys_h, preferred_element_type=jnp.float32
    ) * HD ** (-0.5)
    offsets = WIN - 1 - lax.broadcasted_iota(jnp.int32, (1, 1, keys_win.shape[0]), 2) // frame_rows
    scores = jnp.where(offsets <= reach, scores, -1e30)
    highest = jnp.max(scores, axis=2, keepdims=True)
    expo = jnp.exp(scores - highest)
    chance = (expo / jnp.sum(expo, axis=2, keepdims=True)).astype(jnp.bfloat16)
    result = jnp.einsum("hqk,khd->qhd", chance, values_h, preferred_element_type=jnp.float32)
    return result.reshape(frame_rows, head_count * HD).astype(jnp.bfloat16)


def on_device(
    latents, noise_level, lookback, level_table, w_query, w_key, w_value, gain_query, gain_key
):
    frame_count = noise_level.shape[0]
    row_count, model_width = latents.shape
    frame_rows = row_count // frame_count
    local_cols = w_query.shape[1]
    total_cols = local_cols * lax.axis_size("tp")
    modulation = level_rows(noise_level, level_table)
    shaped = modulate(latents, modulation, frame_count, frame_rows, model_width)
    queries = jnp.dot(shaped, w_query, preferred_element_type=jnp.float32)
    keys_all = jnp.dot(shaped, w_key, preferred_element_type=jnp.float32)
    values_all = jnp.dot(shaped, w_value, preferred_element_type=jnp.float32)
    sums_query, sums_key = lax.psum(
        (jnp.sum(queries * queries, axis=1), jnp.sum(keys_all * keys_all, axis=1)), "tp"
    )
    query_normed = (
        queries * lax.rsqrt(sums_query[:, None] / total_cols + EPSILON) * gain_query
    ).astype(jnp.bfloat16)
    key_normed = (keys_all * lax.rsqrt(sums_key[:, None] / total_cols + EPSILON) * gain_key).astype(
        jnp.bfloat16
    )
    joined = jnp.concatenate([key_normed, values_all.astype(jnp.bfloat16)], 1)
    joined = jnp.concatenate([fetch_behind(joined, frame_count, frame_rows), joined], 0)
    context_keys = joined[:, :local_cols]
    context_values = joined[:, local_cols:]

    def one_frame(frame_index):
        start = frame_index * frame_rows
        query_rows = lax.dynamic_slice_in_dim(query_normed, start, frame_rows, 0)
        key_win = lax.dynamic_slice_in_dim(context_keys, start, WIN * frame_rows, 0)
        value_win = lax.dynamic_slice_in_dim(context_values, start, WIN * frame_rows, 0)
        reach = lax.dynamic_index_in_dim(lookback, frame_index, 0, keepdims=False)
        return window_attend(query_rows, key_win, value_win, reach)

    mixed = lax.map(one_frame, jnp.arange(frame_count, dtype=jnp.int32))
    return mixed.reshape(row_count, local_cols)


def solution(mesh):
    in_specs = (
        P("queue", None),
        P("queue"),
        P("queue"),
        P(),
        P(None, "tp"),
        P(None, "tp"),
        P(None, "tp"),
        P("tp"),
        P("tp"),
    )
    out_specs = P("queue", "tp")
    return jax.shard_map(
        on_device, mesh=mesh, in_specs=in_specs, out_specs=out_specs, check_vma=False
    )
```

profile of v0, /device:TPU:66, one launch (start us, length us, event | category | flops | bytes accessed | tf_op | source)
XLA Modules:
  0.0 126.1 jit_solution(7517193285460031689)
XLA Ops:
  0.0 1.1 copy-done
  1.1 1.4 %fusion.22 = f32[2,10240]{1,0:T(2,128)S(1)} fusion(bf16[32,10240]{1,0:T(8,128)(2,1)S(1)} %copy-done, s32[2]{0:T(128)} %param.12), kind=kOutput, calls=%fused_computation.45 | convolution fusion | flops 1310784 | bytes 737288 | tf_op jit(solution)/shard_map/dot_general | solution.py:24
  2.5 3.3 %convert_reduce_fusion = f32[512]{0:T(512)S(1)} fusion(bf16[512,5120]{1,0:T(8,128)(2,1)} %param.11), kind=kLoop, calls=%fused_computation.27 | loop fusion | flops 5242368 | bytes 5244928 | tf_op jit(solution)/shard_map/reduce_sum | solution.py:29
  5.8 0.0 slice-start
  5.8 1.5 %fusion.18 = f32[512]{0:T(512)S(1)} fusion(bf16[512,5120]{1,0:T(8,128)(2,1)S(1)} %copy-done.1, f32[512]{0:T(512)S(1)} %broadcast_multiply_fusion), kind=kLoop, calls=%fused_computation.30 | loop fusion | flops 10485248 | bytes 5246976 | tf_op jit(solution)/shard_map/reduce_sum | solution.py:30
  7.3 0.0 slice-start.1
  7.3 3.0 %fusion.21 = bf16[512,5120]{1,0:T(8,128)(2,1)S(1)} fusion(bf16[512,5120]{1,0:T(8,128)(2,1)S(1)} %copy-done.1, f32[2,5120]{1,0:T(2,128)S(1)} %get-tuple-element.133, f32[2,5120]{1,0:T(2,128)S(1)} %get-tuple-element.132, f32[512]{0:T(512)S(1)} %add_rsqrt_fusion.2, f32[512]{0:T(512)S(1)} %broadcast_multiply_fusion), kind=kLoop, calls=%fused_computation.33 | loop fusion | flops 15728640 | bytes 10571776 | tf_op jit(solution)/shard_map/convert_element_type | solution.py:35
  10.4 4.4 %multiply_reduce_fusion.1 = (f32[512]{0:T(512)S(1)}, f32[512,640]{1,0:T(8,128)S(1)}) fusion(bf16[512,5120]{1,0:T(8,128)(2,1)S(1)} %fusion.21, bf16[5120,640]{1,0:T(8,128)(2,1)S(1)} %bitcast.48), kind=kOutput, calls=%fused_computation.40 | convolution fusion | flops 3356098048 | bytes 13109248 | tf_op jit(solution)/shard_map/dot_general | solution.py:82
  14.8 7.6 %multiply_reduce_fusion = (f32[512]{0:T(512)S(1)}, f32[512,640]{1,0:T(8,128)}) fusion(bf16[512,5120]{1,0:T(8,128)(2,1)S(1)} %fusion.21, bf16[5120,640]{1,0:T(8,128)(2,1)} %param.15), kind=kOutput, calls=%fused_computation.38 | convolution fusion | flops 3356098048 | bytes 13109248 | tf_op jit(solution)/shard_map/dot_general | solution.py:81
  22.4 8.8 %all-reduce = (f32[512]{0:T(512)S(1)}, f32[512]{0:T(512)S(1)}) all-reduce(f32[512]{0:T(512)S(1)} %get-tuple-element.134, f32[512]{0:T(512)S(1)} %get-tuple-element.136), channel_id=1, replica_groups=mesh['queue'=32,'tp'=4] {'tp'}, use_global_device_ids=true, to_apply=%region_5.0 | all-reduce | flops 1024 | bytes 8192 | tf_op jit(solution)/shard_map/psum | solution.py:84
  31.2 8.7 %convolution_convert_fusion = bf16[512,640]{1,0:T(8,128)(2,1)S(1)} fusion(bf16[512,5120]{1,0:T(8,128)(2,1)} %copy-done.2, bf16[5120,640]{1,0:T(8,128)(2,1)} %param.17), kind=kOutput, calls=%fused_computation.35 | convolution fusion | flops 3355770880 | bytes 12451840 | tf_op jit(solution)/shard_map/dot_general | solution.py:83
  39.8 0.0 copy-start.4
  39.9 0.2 multiply_convert_fusion.1
  40.0 0.1 pad_maximum_fusion
  40.2 1.9 %collective-permute-start = (bf16[512,1280]{1,0:T(8,128)(2,1)S(1)}, bf16[512,1280]{1,0:T(8,128)(2,1)S(1)}, u32[]{:S(2)}, u32[]{:S(2)}) collective-permute-start(bf16[512,1280]{1,0:T(8,128)(2,1)S(1)} %pad_maximum_fusion), channel_id=1, source_target_pairs={{0,4},{4,8},{8,12},{12,16},{16,20},{20,24},{24,28},{28,32},{32,36}... | collective-permute-start | bytes 3932168 | tf_op jit(solution)/shard_map/ppermute | solution.py:16
  42.1 19.1 %collective-permute-done = bf16[512,1280]{1,0:T(8,128)(2,1)S(1)} collective-permute-done((bf16[512,1280]{1,0:T(8,128)(2,1)S(1)}, bf16[512,1280]{1,0:T(8,128)(2,1)S(1)}, u32[]{:S(2)}, u32[]{:S(2)}) %collective-permute-start) | collective-permute-done | bytes 1310752 | tf_op jit(solution)/shard_map/ppermute | solution.py:16
  61.2 0.9 slice.22
  62.1 1.9 %collective-permute-start.1 = (bf16[256,1280]{1,0:T(8,128)(2,1)}, bf16[256,1280]{1,0:T(8,128)(2,1)}, u32[]{:S(2)}, u32[]{:S(2)}) collective-permute-start(bf16[256,1280]{1,0:T(8,128)(2,1)} %slice.22), channel_id=1, source_target_pairs={{0,4},{4,8},{8,12},{12,16},{16,20},{20,24},{24,28},{28,32},{32,36}... | collective-permute-start | bytes 1966088 | tf_op jit(solution)/shard_map/ppermute | solution.py:16
  64.0 2.3 %multiply_convert_fusion = bf16[512,640]{1,0:T(8,128)(2,1)} fusion(f32[512,640]{1,0:T(8,128)} %get-tuple-element.137, f32[640]{0:T(1024)S(1)} %copy-done.4, f32[512]{0:T(512)S(1)} %add_rsqrt_fusion), kind=kLoop, calls=%fused_computation.37 | loop fusion | flops 983040 | bytes 1970688 | tf_op jit(solution)/shard_map/convert_element_type | solution.py:89
  66.4 10.0 %collective-permute-done.1 = bf16[256,1280]{1,0:T(8,128)(2,1)} collective-permute-done((bf16[256,1280]{1,0:T(8,128)(2,1)}, bf16[256,1280]{1,0:T(8,128)(2,1)}, u32[]{:S(2)}, u32[]{:S(2)}) %collective-permute-start.1) | collective-permute-done | bytes 655392 | tf_op jit(solution)/shard_map/ppermute | solution.py:16
  76.4 7.7 %maximum_maximum_fusion = bf16[1280,1280]{1,0:T(8,128)(2,1)S(1)} fusion(bf16[512,640]{1,0:T(8,128)(2,1)S(1)} %convolution_convert_fusion, bf16[512,640]{1,0:T(8,128)(2,1)S(1)} %multiply_convert_fusion.1, bf16[512,1280]{1,0:T(8,128)(2,1)S(1)} %collective-permute-done, bf16[256,1280]{1,0:T(8,128)(2,1)} %collective-permute-done.1), kind=kLoop, calls=%fused_computation.34 | loop fusion | flops 13107200 | bytes 6553600 | tf_op jit(solution)/shard_map/concatenate | solution.py:94
  84.1 2.0 %fusion.27 = (bf16[1280,640]{1,0:T(8,128)(2,1)}, bf16[1280,640]{1,0:T(8,128)(2,1)}) fusion(bf16[1280,1280]{1,0:T(8,128)(2,1)S(1)} %maximum_maximum_fusion), kind=kLoop, calls=%fused_computation.51 | loop fusion | bytes 6553600 | tf_op jit(solution)/shard_map/slice | solution.py:95
  86.1 40.1 %while.12 = (s32[]{:T(128)}, bf16[2,256,640]{2,1,0:T(8,128)(2,1)}, s32[2]{0:T(128)S(1)}, bf16[1280,640]{1,0:T(8,128)(2,1)}, s32[2]{0:T(128)S(1)}, /*index=5*/bf1...) while((s32[]{:T(128)}, bf16[2,256,640]{2,1,0:T(8,128)(2,1)}, ...), condition=%wide.region_9.10_spmd, body=%wide.region_6.9_spmd.sunk | while | flops 679128064 | bytes 32125252 | solution.py:106
  86.1 0.6 dynamic_slice.41
  87.3 1.9 %constant_dynamic-slice_fusion.5 = (bf16[1024,640]{1,0:T(8,128)(2,1)S(1)}, bf16[1024,640]{1,0:T(8,128)(2,1)S(1)}) fusion(bf16[1280,640]{1,0:T(8,128)(2,1)} %get-tuple-element.221, s32[]{:T(128)S(6)} %select_n.62, bf16[1280,640]{1,0:T(8,128)(2,1)} %get-tuple-element.218), kind=kLoop, calls=%fused_computation.21.clone.1 | loop fusion | bytes 5242884 | tf_op jit(solution)/shard_map/while/body/eval_jaxpr/dynamic_slice | solution.py:101
  89.3 1.5 %copy.31 = bf16[1024,640]{0,1:T(8,128)(2,1)} copy(bf16[1024,640]{1,0:T(8,128)(2,1)S(1)} %get-tuple-element.186) | data formatting | bytes 2621440 | tf_op jit(solution)/shard_map/while/body/eval_jaxpr/dynamic_slice | solution.py:101
  90.8 1.0 constant_dynamic-slice_fusion.6
  91.8 0.2 copy.30
  93.9 0.6 dynamic_slice.42
  94.5 0.6 fusion.49
  95.2 5.5 %fusion.50 = (f32[5,256]{1,0:T(8,128)S(1)}, f32[5,256,1024]{2,1,0:T(8,128)}) fusion(pred[1024]{0:T(1024)(128)(4,1)S(1)} %fusion.49, bf16[256,5,128]{0,2,1:T(8,128)(2,1)S(1)} %bitcast.45, bf16[1024,5,128]{0,2,1:T(8,128)(2,1)} %bitcast.43), kind=kOutput, calls=%fused_computation.50.clone.1 | convolution fusion | flops 340788224 | bytes 6887424 | tf_op jit(solution)/shard_map/while/body/eval_jaxpr/sub | solution.py:65
  100.7 0.6 copy.29
  101.3 0.0 copy-start.5
  101.4 3.6 %fusion.51 = bf16[5,128,256]{2,1,0:T(8,128)(2,1)S(1)} fusion(bf16[1024,5,128]{0,2,1:T(8,128)(2,1)S(1)} %bitcast.44, f32[5,256,1024]{2,1,0:T(8,128)} %get-tuple-element.187, f32[5,256]{1,0:T(8,128)S(1)} %get-tuple-element.188), kind=kOutput, calls=%fused_computation.9.clone.1 | convolution fusion | flops 338329600 | bytes 6886400 | tf_op jit(solution)/shard_map/while/body/eval_jaxpr/hqk,khd->qhd/dot_general | solution.py:67
  105.0 0.2 copy.32
  105.3 0.8 copy-done.6
  106.1 0.6 dynamic_slice.41
  107.4 1.9 %constant_dynamic-slice_fusion.5 = (bf16[1024,640]{1,0:T(8,128)(2,1)S(1)}, bf16[1024,640]{1,0:T(8,128)(2,1)S(1)}) fusion(bf16[1280,640]{1,0:T(8,128)(2,1)} %get-tuple-element.221, s32[]{:T(128)S(6)} %select_n.62, bf16[1280,640]{1,0:T(8,128)(2,1)} %get-tuple-element.218), kind=kLoop, calls=%fused_computation.21.clone.1 | loop fusion | bytes 5242884 | tf_op jit(solution)/shard_map/while/body/eval_jaxpr/dynamic_slice | solution.py:101
  109.3 1.5 %copy.31 = bf16[1024,640]{0,1:T(8,128)(2,1)} copy(bf16[1024,640]{1,0:T(8,128)(2,1)S(1)} %get-tuple-element.186) | data formatting | bytes 2621440 | tf_op jit(solution)/shard_map/while/body/eval_jaxpr/dynamic_slice | solution.py:101
  110.8 1.0 constant_dynamic-slice_fusion.6
  111.8 0.2 copy.30
  113.9 0.6 dynamic_slice.42
  114.6 0.6 fusion.49
  115.2 5.5 %fusion.50 = (f32[5,256]{1,0:T(8,128)S(1)}, f32[5,256,1024]{2,1,0:T(8,128)}) fusion(pred[1024]{0:T(1024)(128)(4,1)S(1)} %fusion.49, bf16[256,5,128]{0,2,1:T(8,128)(2,1)S(1)} %bitcast.45, bf16[1024,5,128]{0,2,1:T(8,128)(2,1)} %bitcast.43), kind=kOutput, calls=%fused_computation.50.clone.1 | convolution fusion | flops 340788224 | bytes 6887424 | tf_op jit(solution)/shard_map/while/body/eval_jaxpr/sub | solution.py:65
  120.7 0.6 copy.29
  121.4 3.6 %fusion.51 = bf16[5,128,256]{2,1,0:T(8,128)(2,1)S(1)} fusion(bf16[1024,5,128]{0,2,1:T(8,128)(2,1)S(1)} %bitcast.44, f32[5,256,1024]{2,1,0:T(8,128)} %get-tuple-element.187, f32[5,256]{1,0:T(8,128)S(1)} %get-tuple-element.188), kind=kOutput, calls=%fused_computation.9.clone.1 | convolution fusion | flops 338329600 | bytes 6886400 | tf_op jit(solution)/shard_map/while/body/eval_jaxpr/hqk,khd->qhd/dot_general | solution.py:67
  125.0 0.2 copy.32
  125.3 0.8 copy-done.6
  (27 shorter events, 0.2 us)
Async XLA Ops:
  0.0 1.1 copy-start
  0.0 5.8 %copy-start.1 = (bf16[512,5120]{1,0:T(8,128)(2,1)S(1)}, bf16[512,5120]{1,0:T(8,128)(2,1)}, u32[]{:S(2)}) copy-start(bf16[512,5120]{1,0:T(8,128)(2,1)} %param.11) | copy-start | bytes 15728644
  5.8 4.5 %slice-start = ((s8[6553600]{0:T(1024)(128)(4,1)}), s8[4194304]{0:T(1024)(128)(4,1)S(1)}, s32[]{:S(2)}) async-start(s8[6553600]{0:T(1024)(128)(4,1)} %bitcast.47), calls=%async_computation | async-start | bytes 8388608
  7.3 3.0 %slice-start.1 = ((s8[6553600]{0:T(1024)(128)(4,1)}), s8[2359296]{0:T(1024)(128)(4,1)S(1)}, s32[]{:S(2)}) async-start(s8[6553600]{0:T(1024)(128)(4,1)} %bitcast.47), calls=%async_computation.1 | async-start | bytes 4718592
  10.4 4.4 %copy-start.2 = (bf16[512,5120]{1,0:T(8,128)(2,1)}, bf16[512,5120]{1,0:T(8,128)(2,1)S(1)}, u32[]{:S(2)}) copy-start(bf16[512,5120]{1,0:T(8,128)(2,1)S(1)} %fusion.21) | copy-start | bytes 15728644
  31.2 8.7 %copy-start.3 = (f32[640]{0:T(1024)S(1)}, f32[640]{0:T(1024)}, u32[]{:S(2)}) copy-start(f32[640]{0:T(1024)} %param.19) | copy-start | bytes 7684
  39.8 24.2 %copy-start.4 = (f32[640]{0:T(1024)S(1)}, f32[640]{0:T(1024)}, u32[]{:S(2)}) copy-start(f32[640]{0:T(1024)} %param.18) | copy-start | bytes 7684
  40.2 21.0 %collective-permute-start = (bf16[512,1280]{1,0:T(8,128)(2,1)S(1)}, bf16[512,1280]{1,0:T(8,128)(2,1)S(1)}, u32[]{:S(2)}, u32[]{:S(2)}) collective-permute-start(bf16[512,1280]{1,0:T(8,128)(2,1)S(1)} %pad_maximum_fusion), channel_id=1, source_target_pairs={{0,4},{4,8},{8,12},{12,16},{16,20},{20,24},{24,28},{28,32},{32,36}... | collective-permute-start | bytes 3932168 | tf_op jit(solution)/shard_map/ppermute | solution.py:16
  62.1 14.3 %collective-permute-start.1 = (bf16[256,1280]{1,0:T(8,128)(2,1)}, bf16[256,1280]{1,0:T(8,128)(2,1)}, u32[]{:S(2)}, u32[]{:S(2)}) collective-permute-start(bf16[256,1280]{1,0:T(8,128)(2,1)} %slice.22), channel_id=1, source_target_pairs={{0,4},{4,8},{8,12},{12,16},{16,20},{20,24},{24,28},{28,32},{32,36}... | collective-permute-start | bytes 1966088 | tf_op jit(solution)/shard_map/ppermute | solution.py:16
  66.4 19.7 %copy-start.7 = (s32[2]{0:T(128)S(1)}, s32[2]{0:T(128)}, u32[]{:S(2)}) copy-start(s32[2]{0:T(128)} %param.13) | copy-start | bytes 28
  101.3 3.9 %copy-start.5 = (bf16[2,256,640]{2,1,0:T(8,128)(2,1)S(1)}, bf16[2,256,640]{2,1,0:T(8,128)(2,1)}, u32[]{:S(2)}) copy-start(bf16[2,256,640]{2,1,0:T(8,128)(2,1)} %get-tuple-element.203) | copy-start | bytes 1966084 | tf_op jit(solution)/shard_map/while
  105.3 0.8 copy-start.6
  121.4 3.9 %copy-start.5 = (bf16[2,256,640]{2,1,0:T(8,128)(2,1)S(1)}, bf16[2,256,640]{2,1,0:T(8,128)(2,1)}, u32[]{:S(2)}) copy-start(bf16[2,256,640]{2,1,0:T(8,128)(2,1)} %get-tuple-element.203) | copy-start | bytes 1966084 | tf_op jit(solution)/shard_map/while
  125.3 0.8 copy-start.6
where the time goes:
time: 129 us; the launch traced here: 126 us
  matrix products  40.4 us (31%)
  waiting for transfers between devices  29.1 us (23%)
  other arithmetic  19.4 us (15%)
  local copies, waits for them, and re-layouts  19.2 us (15%)
  blocking collectives  8.77 us (7%)
  loops' own time  5.26 us (4%)
  starting transfers between devices  3.83 us (3%)
    ppermute x2, waiting for transfers between devices, passed_along(): return lax.ppermute(x, axis, pairs)  29.1 us
    sub x2, matrix products, window_attend(): expo = jnp.exp(scores - highest)  11.1 us
    psum x1, blocking collectives, on_device(): lax.psum((jnp.sum(queries * queries, axis=1), jnp.sum(keys_all * keys_all...  8.77 us
    dot_general x1, matrix products, on_device(): values_all = jnp.dot(shaped, w_value, preferred_element_type=jnp.float32)  8.65 us
    concatenate x1, other arithmetic, on_device(): jnp.concatenate([fetch_behind(joined, frame_count, frame_rows), joined], 0)  7.66 us
    dot_general x1, matrix products, on_device(): queries = jnp.dot(shaped, w_query, preferred_element_type=jnp.float32)  7.64 us
    dot_general x2, matrix products, window_attend(): jnp.einsum('hqk,khd->qhd', chance, values_h, preferred_element_type=jnp.f...  7.26 us
    dynamic_slice x4, local copies, waits for them, and re-layouts, one_frame(): key_win = lax.dynamic_slice_in_dim(context_keys, start, WIN * frame_rows, 0)  6.97 us
  transfers between devices with their start and end apart: 2, of which 2 were waited for; matrix products, arithmetic and copies ran while one was open for 2% of the time, Pallas kernels for 0%

commit v1 on v0

v1 whole, which is shorter than its diff:
```python
import functools

import jax
import jax.numpy as jnp
from jax import lax
from jax.experimental import pallas as pl
from jax.experimental.pallas import tpu as pltpu
from jax.sharding import PartitionSpec as P

HD = 128
WIN = 4
EPSILON = 1e-06
MIB = 2**20
EXP2_SCALE = HD ** (-0.5) * 1.4426950408889634

HBM = pl.BlockSpec(memory_space=pltpu.HBM)
VMEM = pl.BlockSpec(memory_space=pltpu.VMEM)
SMEM = pl.BlockSpec(memory_space=pltpu.SMEM)


def as_rows(column):
    wide = jnp.broadcast_to(column, (column.shape[0], 128))
    parts = [
        jnp.transpose(wide[i : i + 128])[0:1] for i in range(0, column.shape[0], 128)
    ]
    return jnp.concatenate(parts, 0)


def as_columns(rows):
    parts = [
        jnp.transpose(jnp.broadcast_to(rows[i : i + 1], (128, 128)))
        for i in range(rows.shape[0])
    ]
    return jnp.concatenate(parts, 0)


def value_kernel(
    noise_level, lookback, latents, level_table, w_query, w_key, w_value, gain_query, gain_key,
    shaped, key_weights, mixed_weights, value_both, value_early, gains_query, gains_key, info,
    levels, reaches, lat, weights, table, shift, scale, small_sem, lat_sem, w_sem,
):
    width = latents.shape[1]
    frame = latents.shape[0] // 2
    half = frame // 2
    cols = w_value.shape[1]
    main = key_weights.shape[1]
    rest = cols - main
    small = [
        pltpu.make_async_copy(src, dst, small_sem.at[i])
        for i, (src, dst) in enumerate(
            (
                (noise_level, levels),
                (level_table, table),
                (lookback, reaches),
                (gain_query, gains_query.at[0]),
                (gain_key, gains_key.at[0]),
            )
        )
    ]
    lat_copies = [
        pltpu.make_async_copy(
            latents.at[pl.ds(c * half, half)], lat.at[pl.ds(c * half, half)], lat_sem.at[c]
        )
        for c in range(4)
    ]
    for copy in small[:2] + lat_copies + small[2:]:
        copy.start()
    bounds = (0, 256, 640)
    fetches = [
        pltpu.make_async_copy(src, dst, w_sem.at[i])
        for i, (src, dst) in enumerate(
            (
                (w_value.at[:, pl.ds(0, 256)], weights.at[:, pl.ds(0, 256)]),
                (w_value.at[:, pl.ds(256, 384)], weights.at[:, pl.ds(256, 384)]),
                (w_key.at[:, pl.ds(0, main)], key_weights),
                (w_key.at[:, pl.ds(main, rest)], mixed_weights.at[:, pl.ds(0, rest)]),
                (w_query.at[:, pl.ds(0, rest)], mixed_weights.at[:, pl.ds(rest, rest)]),
            )
        )
    ]

    for copy in small[:2]:
        copy.wait()
    for f in range(2):
        chosen = lax.broadcasted_iota(jnp.int32, (table.shape[0], 1), 0) == levels[f]
        row = jnp.sum(jnp.where(chosen, table[...].astype(jnp.float32), 0.0), axis=0, keepdims=True)
        shift[f : f + 1, :] = row[:, :width]
        scale[f : f + 1, :] = 1.0 + row[:, width:]

    group = 64
    for c in range(4):
        lat_copies[c].wait()
        if c >= 1:
            fetches[c - 1].start()
        f = c // 2
        for start in range(c * half, (c + 1) * half, group):
            rows = slice(start, start + group)
            x = lat[rows, :].astype(jnp.float32)
            center = jnp.mean(x, axis=1, keepdims=True)
            x = x - center
            spread = jnp.mean(x * x, axis=1, keepdims=True)
            x = x * lax.rsqrt(spread + EPSILON)
            shaped[rows, :] = (x * scale[f : f + 1, :] + shift[f : f + 1, :]).astype(jnp.bfloat16)

    fetches[3].start()
    fetches[4].start()
    for i, (s, e) in enumerate(zip(bounds, bounds[1:])):
        fetches[i].wait()
        result = jnp.dot(shaped[...], weights[:, s:e], preferred_element_type=jnp.float32)
        turned = jnp.transpose(result).astype(jnp.bfloat16)
        value_both[s:e, :] = turned
        value_early[s:e, :] = turned[:, frame:]
    for copy in small[2:]:
        copy.wait()
    info[0] = reaches[0]
    info[1] = reaches[1]
    info[2] = lax.rem(lax.axis_index("queue"), 2)
    for copy in fetches[2:]:
        copy.wait()


def project_value(noise_level, lookback, latents, level_table, w_query, w_key, w_value, gain_query, gain_key):
    rows, width = latents.shape
    cols = w_query.shape[1]
    half = rows // 2
    main = cols // 256 * 256
    f32, bf16 = jnp.float32, jnp.bfloat16
    operands = (
        noise_level, lookback, latents, level_table, w_query, w_key, w_value, gain_query, gain_key
    )
    operands = [pltpu.with_memory_space_constraint(x, pltpu.HBM) for x in operands]
    return pl.pallas_call(
        value_kernel,
        out_shape=(
            pltpu.VMEM((rows, width), bf16),
            pltpu.VMEM((width, main), bf16),
            pltpu.VMEM((width, 2 * (cols - main)), bf16),
            pltpu.VMEM((cols, rows), bf16),
            pltpu.VMEM((cols, half), bf16),
            pltpu.VMEM((1, cols), f32),
            pltpu.VMEM((1, cols), f32),
            pltpu.SMEM((3,), jnp.int32),
        ),
        in_specs=[HBM] * 9,
        out_specs=(VMEM,) * 7 + (SMEM,),
        scratch_shapes=[
            pltpu.SMEM((2,), jnp.int32),
            pltpu.SMEM((2,), jnp.int32),
            pltpu.VMEM((rows, width), bf16),
            pltpu.VMEM((width, cols), bf16),
            pltpu.VMEM(level_table.shape, bf16),
            pltpu.VMEM((2, width), f32),
            pltpu.VMEM((2, width), f32),
            pltpu.SemaphoreType.DMA((5,)),
            pltpu.SemaphoreType.DMA((4,)),
            pltpu.SemaphoreType.DMA((5,)),
        ],
        compiler_params=pltpu.CompilerParams(vmem_limit_bytes=18 * MIB),
        cost_estimate=pl.CostEstimate(
            flops=2 * rows * width * cols, bytes_accessed=26_000_000, transcendentals=0
        ),
        name="project_value",
    )(*operands)


def query_key_kernel(shaped, key_weights, mixed_weights, w_query, query, key, sums_out, weights, sem):
    cols = query.shape[1]
    main = key_weights.shape[1]
    rest = cols - main
    fetch = pltpu.make_async_copy(w_query.at[:, pl.ds(rest, main)], weights, sem.at[0])
    fetch.start()

    def dot(w):
        return jnp.dot(shaped[...], w[...], preferred_element_type=jnp.float32)

    key[:, :main] = dot(key_weights)
    middle = dot(mixed_weights)
    key[:, main:] = middle[:, :rest]
    query[:, :rest] = middle[:, rest:]
    fetch.wait()
    query[:, rest:] = dot(weights)
    for at, ref in ((0, key), (4, query)):
        x = ref[...]
        sums_out[at : at + 4, :] = as_rows(jnp.sum(x * x, axis=1, keepdims=True))


def project_query_key(shaped, key_weights, mixed_weights, w_query):
    rows, width = shaped.shape
    cols = w_query.shape[1]
    f32 = jnp.float32
    return pl.pallas_call(
        query_key_kernel,
        out_shape=(
            pltpu.VMEM((rows, cols), f32),
            pltpu.VMEM((rows, cols), f32),
            pltpu.VMEM((8, 128), f32),
        ),
        in_specs=[VMEM] * 3 + [HBM],
        out_specs=(VMEM,) * 3,
        scratch_shapes=[pltpu.VMEM(key_weights.shape, jnp.bfloat16), pltpu.SemaphoreType.DMA((1,))],
        compiler_params=pltpu.CompilerParams(vmem_limit_bytes=16 * MIB),
        cost_estimate=pl.CostEstimate(
            flops=4 * rows * width * cols, bytes_accessed=18_000_000, transcendentals=0
        ),
        name="project_query_key",
    )(shaped, key_weights, mixed_weights, pltpu.with_memory_space_constraint(w_query, pltpu.HBM))


def norm_factor(sums, at, total_cols):
    first, second, third, fourth = (x[at : at + 4, :] for x in sums)
    return as_columns(lax.rsqrt((first + second + (third + fourth)) / total_cols + EPSILON))


def key_kernel(total_cols, key, gain, s0, s1, s2, s3, all_out, early, late):
    factor = norm_factor((s0, s1, s2, s3), 0, total_cols)
    half = late.shape[0]
    for c in range(0, key.shape[1], 128):
        normed = (key[:, c : c + 128] * factor * gain[0:1, c : c + 128]).astype(jnp.bfloat16)
        all_out[:, c : c + 128] = normed
        late[:, c : c + 128] = normed[:half]
        early[:, c : c + 128] = normed[half:]


def normalise_key(key, gain, sums, total_cols):
    rows, cols = key.shape
    bf16 = jnp.bfloat16
    return pl.pallas_call(
        functools.partial(key_kernel, total_cols),
        out_shape=(
            jax.ShapeDtypeStruct((rows, cols), bf16),
            jax.ShapeDtypeStruct((rows // 2, cols), bf16),
            jax.ShapeDtypeStruct((rows // 2, cols), bf16),
        ),
        in_specs=[VMEM] * 6,
        out_specs=(VMEM,) * 3,
        compiler_params=pltpu.CompilerParams(vmem_limit_bytes=12 * MIB),
        cost_estimate=pl.CostEstimate(flops=2 * rows * cols, bytes_accessed=100_000, transcendentals=0),
        name="normalise_key",
    )(key, gain, *sums)


def attend_block(first, q, k, vt, acc, peak, mass):
    heads = q.shape[1] // HD
    cols = [slice(h * HD, (h + 1) * HD) for h in range(heads)]
    scores = [
        lax.dot_general(k[:, c], q[:, c], (((1,), (1,)), ((), ())), preferred_element_type=jnp.float32)
        for c in cols
    ]
    tops = [jnp.max(s, axis=0, keepdims=True) for s in scores]
    if not first:
        olds = [peak[h : h + 1, :] for h in range(heads)]
        tops = [jnp.maximum(t, o) for t, o in zip(tops, olds)]
        fades = [jnp.exp2((o - t) * EXP2_SCALE) for t, o in zip(tops, olds)]
    expos = [jnp.exp2((s - t) * EXP2_SCALE) for s, t in zip(scores, tops)]
    for h in range(heads):
        total = jnp.sum(expos[h], axis=0, keepdims=True)
        peak[h : h + 1, :] = tops[h]
        mass[h : h + 1, :] = total if first else mass[h : h + 1, :] * fades[h] + total
    for h, c in enumerate(cols):
        part = jnp.dot(vt[c, :], expos[h].astype(jnp.bfloat16), preferred_element_type=jnp.float32)
        acc[c, :] = part if first else acc[c, :] * fades[h] + part


def local_kernel(
    total_cols, info, query, gain, s0, s1, s2, s3, key, value, pair_key_0, pair_key_1, pair_value,
    query_out, acc, peak, mass,
):
    factor = norm_factor((s0, s1, s2, s3), 4, total_cols)
    for c in range(0, query.shape[1], 128):
        query_out[:, c : c + 128] = (
            query[:, c : c + 128] * factor * gain[0:1, c : c + 128]
        ).astype(jnp.bfloat16)
    frame = query.shape[0] // 2
    at = [pl.ds(0, frame), pl.ds(frame, frame)]
    for f in range(2):
        parts = (acc.at[f], peak.at[f], mass.at[f])
        q = query_out.at[at[f]]
        attend_block(True, q, key.at[at[f]], value.at[:, at[f]], *parts)
        if f == 1:

            @pl.when(info[f] >= 1)
            def _():
                attend_block(False, q, key.at[at[0]], value.at[:, at[0]], *parts)

        for g, k in ((0, pair_key_0), (1, pair_key_1)):

            @pl.when(jnp.logical_and(info[2] == 1, info[f] >= f + 2 - g))
            def _():
                attend_block(False, q, k, pair_value.at[:, at[g]], *parts)


def local_attention(info, query, gain, sums, key, value, pairs, total_cols):
    rows, cols = query.shape
    f32 = jnp.float32
    stats = jax.ShapeDtypeStruct((2, 8, rows // 2), f32)
    return pl.pallas_call(
        functools.partial(local_kernel, total_cols),
        out_shape=(
            jax.ShapeDtypeStruct((rows, cols), jnp.bfloat16),
            jax.ShapeDtypeStruct((2, cols, rows // 2), f32),
            stats,
            stats,
        ),
        in_specs=[SMEM] + [VMEM] * 11,
        out_specs=(VMEM,) * 4,
        compiler_params=pltpu.CompilerParams(vmem_limit_bytes=12 * MIB),
        cost_estimate=pl.CostEstimate(flops=3_000_000, bytes_accessed=100_000, transcendentals=0),
        name="local_attention",
    )(info, query, gain, *sums, key, value, *pairs)


def near_kernel(info, query, acc_in, peak_in, mass_in, mid_keys, near_keys, values, acc, peak, mass):
    keys = (mid_keys, near_keys)
    frame = query.shape[0] // 2
    at = [pl.ds(0, frame), pl.ds(frame, frame)]
    acc[...] = acc_in[...]
    peak[...] = peak_in[...]
    mass[...] = mass_in[...]
    for f, reach, g in ((0, 1, 1), (0, 2, 0), (1, 2, 1), (1, 3, 0)):

        @pl.when(jnp.logical_and(info[2] == 0, info[f] >= reach))
        def _():
            attend_block(
                False, query.at[at[f]], keys[g], values.at[:, at[g]],
                acc.at[f], peak.at[f], mass.at[f],
            )


def near_attention(info, query, acc, peak, mass, mid_keys, near_keys, values):
    rows, cols = query.shape
    f32 = jnp.float32
    stats = jax.ShapeDtypeStruct((2, 8, rows // 2), f32)
    return pl.pallas_call(
        near_kernel,
        out_shape=(jax.ShapeDtypeStruct((2, cols, rows // 2), f32), stats, stats),
        in_specs=[SMEM] + [VMEM] * 7,
        out_specs=(VMEM,) * 3,
        compiler_params=pltpu.CompilerParams(vmem_limit_bytes=12 * MIB),
        cost_estimate=pl.CostEstimate(flops=1_000_000, bytes_accessed=100_000, transcendentals=0),
        name="near_attention",
    )(info, query, acc, peak, mass, mid_keys, near_keys, values)


def far_kernel(
    info, query, acc_in, peak_in, mass_in, far_keys, far_values, relayed_keys, relayed_values,
    out, acc, peak, mass,
):
    cols = query.shape[1]
    frame = query.shape[0] // 2
    at = [pl.ds(0, frame), pl.ds(frame, frame)]
    acc[...] = acc_in[0]
    peak[...] = peak_in[0]
    mass[...] = mass_in[0]
    for core, k, v in (
        (0, far_keys, far_values),
        (1, relayed_keys, relayed_values.at[:, at[1]]),
    ):

        @pl.when(jnp.logical_and(info[2] == core, info[0] >= 3))
        def _():
            attend_block(False, query.at[at[0]], k, v, acc, peak, mass)

    for f in range(2):
        for h in range(cols // HD):
            c = slice(h * HD, (h + 1) * HD)
            if f == 0:
                result = acc[c, :] / mass[h : h + 1, :]
            else:
                result = acc_in[f, c, :] / mass_in[f, h : h + 1, :]
            out[at[f], c] = jnp.transpose(result).astype(out.dtype)


def far_attention(info, query, acc, peak, mass, halo):
    rows, cols = query.shape
    f32 = jnp.float32
    stats = pltpu.VMEM((8, rows // 2), f32)
    return pl.pallas_call(
        far_kernel,
        out_shape=jax.ShapeDtypeStruct((rows, cols), jnp.bfloat16),
        in_specs=[SMEM] + [VMEM] * 8,
        out_specs=VMEM,
        scratch_shapes=[pltpu.VMEM((cols, rows // 2), f32), stats, stats],
        compiler_params=pltpu.CompilerParams(vmem_limit_bytes=12 * MIB),
        cost_estimate=pl.CostEstimate(flops=1_000_000, bytes_accessed=100_000, transcendentals=0),
        name="far_attention",
    )(info, query, acc, peak, mass, *halo)


def on_device(
    latents, noise_level, lookback, level_table, w_query, w_key, w_value, gain_query, gain_key
):
    devices = lax.axis_size("queue")
    total_cols = w_query.shape[1] * lax.axis_size("tp")
    along = [(i, (i + 1) % devices) for i in range(devices)]
    swap = [(i, i ^ 1) for i in range(devices)]

    def move(x, pairs):
        return lax.ppermute(x, "queue", pairs)

    shaped, key_weights, mixed_weights, value, value_early, gain_query, gain_key, info = project_value(
        noise_level, lookback, latents, level_table, w_query, w_key, w_value,
        gain_query, gain_key,
    )
    info = pltpu.with_memory_space_constraint(info, pltpu.SMEM)
    near_value = move(value, along)
    far_value = move(move(value_early, swap), along)
    query, key, sums = project_query_key(shaped, key_weights, mixed_weights, w_query)
    sums = [sums] + [
        lax.ppermute(sums, "tp", pairs)
        for pairs in (
            [(0, 1), (1, 0), (2, 3), (3, 2)],
            [(0, 3), (3, 0), (1, 2), (2, 1)],
            [(0, 2), (2, 0), (1, 3), (3, 1)],
        )
    ]
    key_normed, key_early, key_late = normalise_key(key, gain_key, sums, total_cols)
    key_normed, far_value, near_value = lax.optimization_barrier((key_normed, far_value, near_value))
    relayed_value = move(near_value, swap)
    near_key = move(key_early, along)
    mid_key = move(key_late, along)
    pair_key_1 = move(key_early, swap)
    pair_key_0 = move(key_late, swap)
    far_key = move(pair_key_1, along)
    query_normed, acc, peak, mass = local_attention(
        info, query, gain_query, sums, key_normed, value, (pair_key_0, pair_key_1, near_value), total_cols
    )
    near_key, acc = lax.optimization_barrier((near_key, acc))
    relayed_key = move(near_key, swap)
    acc, peak, mass = near_attention(info, query_normed, acc, peak, mass, mid_key, near_key, near_value)
    return far_attention(
        info, query_normed, acc, peak, mass, (far_key, far_value, relayed_key, relayed_value)
    )


def solution(mesh):
    in_specs = (
        P("queue", None),
        P("queue"),
        P("queue"),
        P(),
        P(None, "tp"),
        P(None, "tp"),
        P(None, "tp"),
        P("tp"),
        P("tp"),
    )
    return jax.shard_map(
        on_device, mesh=mesh, in_specs=in_specs, out_specs=P("queue", "tp"), check_vma=False
    )
```

time: 129 us -> 49.1 us (0.38)
  the two profiles are of different devices: /device:TPU:66 before, /device:TPU:0 now
where the time goes in v1:
time: 49.1 us; the launch traced here: 49 us
  Pallas kernels  22.5 us (46%)
  waiting for transfers between devices  17.4 us (35%)
  starting transfers between devices  9.06 us (18%)
    ppermute x10, waiting for transfers between devices, move(): return lax.ppermute(x, 'queue', pairs)  13.8 us
    pallas_call x1, Pallas kernels, project_value(): pl.pallas_call(value_kernel, out_shape=(pltpu.VMEM((rows, width), bf16),...  11.8 us
    pallas_call x1, Pallas kernels, project_query_key(): pl.pallas_call(query_key_kernel, out_shape=(pltpu.VMEM((rows, cols), f32)...  7.42 us
    ppermute x10, starting transfers between devices, move(): return lax.ppermute(x, 'queue', pairs)  4.82 us
    ppermute x3, starting transfers between devices, on_device(): lax.ppermute(sums, 'tp', pairs)  4.24 us
    ppermute x3, waiting for transfers between devices, on_device(): lax.ppermute(sums, 'tp', pairs)  3.68 us
    pallas_call x1, Pallas kernels, local_attention(): pl.pallas_call(functools.partial(local_kernel, total_cols), out_shape=(ja...  1.55 us
    pallas_call x1, Pallas kernels, far_attention(): pl.pallas_call(far_kernel, out_shape=jax.ShapeDtypeStruct((rows, cols), j...  1.14 us
  transfers between devices with their start and end apart: 13, of which 6 were waited for; matrix products, arithmetic and copies ran while one was open for 0% of the time, Pallas kernels for 20%

profile of v1, /device:TPU:0, one launch (start us, length us, event | category | flops | bytes accessed | tf_op | source)
XLA Modules:
  0.0 49.0 jit_solution(5048946571511003788)
XLA Ops:
  0.0 11.8 %project_value.1 = (bf16[512,5120]{1,0:T(8,128)(2,1)S(1)}, bf16[5120,512]{1,0:T(8,128)(2,1)S(1)}, bf16[5120,256]{1,0:T(8,128)(2,1)S(1)}, bf16[640,512]{1,0:T(8,1...) custom-call(s32[2]{0:T(128)} %noise_level.1, ...), custom_call_target="tpu_custom_call" | custom-call | flops 3355443200 | bytes 26000000 | tf_op jit(solution)/shard_map/project_value/pallas_call | solution.py:132
  11.8 0.1 collective-permute-start.3
  11.9 0.5 %collective-permute-start.5 = (bf16[640,512]{1,0:T(8,128)(2,1)S(1)}, bf16[640,512]{1,0:T(8,128)(2,1)S(1)}, u32[]{:S(2)}, u32[]{:S(2)}) collective-permute-start(bf16[640,512]{1,0:T(8,128)(2,1)S(1)} %get-tuple-element.42.value), channel_id=1, source_target_pairs={{0,4},{4,8},{8,12},{12,16},{16,20},{20,24},{24,28},{28,32},{32,36}... | collective-permute-start | bytes 1966088 | tf_op jit(solution)/shard_map/ppermute | solution.py:398
  12.4 1.1 %collective-permute-done.3 = bf16[640,256]{1,0:T(8,128)(2,1)S(1)} collective-permute-done((bf16[640,256]{1,0:T(8,128)(2,1)S(1)}, bf16[640,256]{1,0:T(8,128)(2,1)S(1)}, u32[]{:S(2)}, u32[]{:S(2)}) %collective-permute-start.3) | collective-permute-done | bytes 327712 | tf_op jit(solution)/shard_map/ppermute | solution.py:398
  13.5 0.2 collective-permute-start.4
  13.7 7.4 %project_query_key.1 = (f32[512,640]{1,0:T(8,128)S(1)}, f32[512,640]{1,0:T(8,128)S(1)}, f32[8,128]{1,0:T(8,128)S(1)}) custom-call(bf16[512,5120]{1,0:T(8,128)(2,1)S(1)} %get-tuple-element.32.shaped, bf16[5120,512]{1,0:T(8,128)(2,1)S(1)} %get-tuple-element.33.key_weights, bf16[5120,256]{1,0:T(8,128)(2,1)S(1)} %get-tuple-element.34.mixed_weights, ...), custom_call_target="tpu_custom_call" | custom-call | flops 6710886400 | bytes 18000000 | tf_op jit(solution)/shard_map/project_query_key/pallas_call | solution.py:191
  21.2 3.1 %collective-permute-start.2 = (f32[8,128]{1,0:T(8,128)S(1)}, f32[8,128]{1,0:T(8,128)S(1)}, u32[]{:S(2)}, u32[]{:S(2)}) collective-permute-start(f32[8,128]{1,0:T(8,128)S(1)} %get-tuple-element.37.s0), channel_id=1, source_target_pairs={{0,2},{2,0},{1,3},{3,1},{4,6},{6,4},{5,7},{7,5},{8,10},{10,8},{9,1... | collective-permute-start | bytes 12296 | tf_op jit(solution)/shard_map/ppermute | solution.py:409
  24.3 1.1 %collective-permute-start.1 = (f32[8,128]{1,0:T(8,128)S(1)}, f32[8,128]{1,0:T(8,128)S(1)}, u32[]{:S(2)}, u32[]{:S(2)}) collective-permute-start(f32[8,128]{1,0:T(8,128)S(1)} %get-tuple-element.37.s0), channel_id=1, source_target_pairs={{0,3},{3,0},{1,2},{2,1},{4,7},{7,4},{5,6},{6,5},{8,11},{11,8},{9,1... | collective-permute-start | bytes 12296 | tf_op jit(solution)/shard_map/ppermute | solution.py:409
  25.4 0.0 collective-permute-start
  25.4 0.9 %collective-permute-done.2.s3 = f32[8,128]{1,0:T(8,128)S(1)} collective-permute-done((f32[8,128]{1,0:T(8,128)S(1)}, f32[8,128]{1,0:T(8,128)S(1)}, u32[]{:S(2)}, u32[]{:S(2)}) %collective-permute-start.2) | collective-permute-done | bytes 4128 | tf_op jit(solution)/shard_map/ppermute | solution.py:409
  26.4 2.7 %collective-permute-done.1.s2 = f32[8,128]{1,0:T(8,128)S(1)} collective-permute-done((f32[8,128]{1,0:T(8,128)S(1)}, f32[8,128]{1,0:T(8,128)S(1)}, u32[]{:S(2)}, u32[]{:S(2)}) %collective-permute-start.1) | collective-permute-done | bytes 4128 | tf_op jit(solution)/shard_map/ppermute | solution.py:409
  29.1 0.0 collective-permute-done.s1
  29.1 0.3 normalise_key.1
  29.3 0.5 collective-permute-start.7
  29.8 0.1 collective-permute-start.6
  29.9 0.4 collective-permute-start.8
  30.3 0.0 collective-permute-done.4.far_values
  30.3 0.0 collective-permute-done.5.pair_value.values
  30.4 1.3 %collective-permute-start.12 = (bf16[640,512]{1,0:T(8,128)(2,1)S(1)}, bf16[640,512]{1,0:T(8,128)(2,1)S(1)}, u32[]{:S(2)}, u32[]{:S(2)}) collective-permute-start(bf16[640,512]{1,0:T(8,128)(2,1)S(1)} %collective-permute-done.5.pair_value.values), channel_id=1, source_target_pairs={{0,4},{4,0},{8,12},{12,8},{16,20},{20,16},{24,28},{28,24},{32,36},... | collective-permute-start | bytes 1966088 | tf_op jit(solution)/shard_map/ppermute | solution.py:398
  31.6 0.1 collective-permute-start.9
  31.7 0.0 collective-permute-done.7.pair_key_1
  31.7 1.6 %collective-permute-start.10 = (bf16[256,640]{1,0:T(8,128)(2,1)S(1)}, bf16[256,640]{1,0:T(8,128)(2,1)S(1)}, u32[]{:S(2)}, u32[]{:S(2)}) collective-permute-start(bf16[256,640]{1,0:T(8,128)(2,1)S(1)} %collective-permute-done.7.pair_key_1), channel_id=1, source_target_pairs={{0,4},{4,8},{8,12},{12,16},{16,20},{20,24},{24,28},{28,32},{32,36}... | collective-permute-start | bytes 983048 | tf_op jit(solution)/shard_map/ppermute | solution.py:398
  33.4 0.0 collective-permute-done.6.pair_key_0
  33.4 1.6 %local_attention.1 = (bf16[512,640]{1,0:T(8,128)(2,1)S(1)}, f32[2,640,256]{2,1,0:T(8,128)S(1)}, f32[2,8,256]{2,1,0:T(8,128)S(1)}, f32[2,8,256]{2,1,0:T(8,128)S(1)}) custom-call(s32[3]{0:T(128)S(4)} %get-tuple-element.31.info, f32[512,640]{1,0:T(8,128)S(1)} %get-tuple-element.35.query, f32[1,640]{1,0:T(1,128)S(1)} %get-tuple-element.36.gain, ...), custom_call_target="tpu_custom_call" | custom-call | flops 3000000 | bytes 100000 | tf_op jit(solution)/shard_map/local_attention/pallas_call | solution.py:296
  34.9 5.9 %collective-permute-done.8.near_keys = bf16[256,640]{1,0:T(8,128)(2,1)S(1)} collective-permute-done((bf16[256,640]{1,0:T(8,128)(2,1)S(1)}, bf16[256,640]{1,0:T(8,128)(2,1)S(1)}, u32[]{:S(2)}, u32[]{:S(2)}) %collective-permute-start.8) | collective-permute-done | bytes 327712 | tf_op jit(solution)/shard_map/ppermute | solution.py:398
  40.9 0.0 collective-permute-start.11
  40.9 3.5 %collective-permute-done.9.mid_keys = bf16[256,640]{1,0:T(8,128)(2,1)S(1)} collective-permute-done((bf16[256,640]{1,0:T(8,128)(2,1)S(1)}, bf16[256,640]{1,0:T(8,128)(2,1)S(1)}, u32[]{:S(2)}, u32[]{:S(2)}) %collective-permute-start.9) | collective-permute-done | bytes 327712 | tf_op jit(solution)/shard_map/ppermute | solution.py:398
  44.4 0.3 near_attention.1
  44.7 3.2 %collective-permute-done.10.far_keys = bf16[256,640]{1,0:T(8,128)(2,1)S(1)} collective-permute-done((bf16[256,640]{1,0:T(8,128)(2,1)S(1)}, bf16[256,640]{1,0:T(8,128)(2,1)S(1)}, u32[]{:S(2)}, u32[]{:S(2)}) %collective-permute-start.10) | collective-permute-done | bytes 327712 | tf_op jit(solution)/shard_map/ppermute | solution.py:398
  47.9 0.0 collective-permute-done.11.relayed_keys
  47.9 0.0 collective-permute-done.12.relayed_values
  47.9 1.1 %far_attention.1 = bf16[512,640]{1,0:T(8,128)(2,1)} custom-call(s32[3]{0:T(128)S(4)} %get-tuple-element.31.info, bf16[512,640]{1,0:T(8,128)(2,1)S(1)} %get-tuple-element.47.query, f32[2,640,256]{2,1,0:T(8,128)S(1)} %get-tuple-element.53.acc_in, f32[2,8,256]{2,1,0:T(8,128)S(1)} %get-tuple-element.54.peak_in, f32[2,8,256]{2,1,0:T(8,128)S(1)} %get-tuple-element.55.mass_in, ...), custom_call_target="tpu_custom_call" | custom-call | flops 1000000 | bytes 100000 | tf_op jit(solution)/shard_map/far_attention/pallas_call | solution.py:377
Async XLA Ops:
  11.8 1.7 %collective-permute-start.3 = (bf16[640,256]{1,0:T(8,128)(2,1)S(1)}, bf16[640,256]{1,0:T(8,128)(2,1)S(1)}, u32[]{:S(2)}, u32[]{:S(2)}) collective-permute-start(bf16[640,256]{1,0:T(8,128)(2,1)S(1)} %get-tuple-element.41), channel_id=1, source_target_pairs={{0,4},{4,0},{8,12},{12,8},{16,20},{20,16},{24,28},{28,24},{32,36},... | collective-permute-start | bytes 983048 | tf_op jit(solution)/shard_map/ppermute | solution.py:398
  11.9 18.5 %collective-permute-start.5 = (bf16[640,512]{1,0:T(8,128)(2,1)S(1)}, bf16[640,512]{1,0:T(8,128)(2,1)S(1)}, u32[]{:S(2)}, u32[]{:S(2)}) collective-permute-start(bf16[640,512]{1,0:T(8,128)(2,1)S(1)} %get-tuple-element.42.value), channel_id=1, source_target_pairs={{0,4},{4,8},{8,12},{12,16},{16,20},{20,24},{24,28},{28,32},{32,36}... | collective-permute-start | bytes 1966088 | tf_op jit(solution)/shard_map/ppermute | solution.py:398
  13.5 16.8 %collective-permute-start.4 = (bf16[640,256]{1,0:T(8,128)(2,1)S(1)}, bf16[640,256]{1,0:T(8,128)(2,1)S(1)}, u32[]{:S(2)}, u32[]{:S(2)}) collective-permute-start(bf16[640,256]{1,0:T(8,128)(2,1)S(1)} %collective-permute-done.3), channel_id=1, source_target_pairs={{0,4},{4,8},{8,12},{12,16},{16,20},{20,24},{24,28},{28,32},{32,36}... | collective-permute-start | bytes 983048 | tf_op jit(solution)/shard_map/ppermute | solution.py:398
  21.2 5.2 %collective-permute-start.2 = (f32[8,128]{1,0:T(8,128)S(1)}, f32[8,128]{1,0:T(8,128)S(1)}, u32[]{:S(2)}, u32[]{:S(2)}) collective-permute-start(f32[8,128]{1,0:T(8,128)S(1)} %get-tuple-element.37.s0), channel_id=1, source_target_pairs={{0,2},{2,0},{1,3},{3,1},{4,6},{6,4},{5,7},{7,5},{8,10},{10,8},{9,1... | collective-permute-start | bytes 12296 | tf_op jit(solution)/shard_map/ppermute | solution.py:409
  24.3 4.8 %collective-permute-start.1 = (f32[8,128]{1,0:T(8,128)S(1)}, f32[8,128]{1,0:T(8,128)S(1)}, u32[]{:S(2)}, u32[]{:S(2)}) collective-permute-start(f32[8,128]{1,0:T(8,128)S(1)} %get-tuple-element.37.s0), channel_id=1, source_target_pairs={{0,3},{3,0},{1,2},{2,1},{4,7},{7,4},{5,6},{6,5},{8,11},{11,8},{9,1... | collective-permute-start | bytes 12296 | tf_op jit(solution)/shard_map/ppermute | solution.py:409
  25.4 3.7 %collective-permute-start = (f32[8,128]{1,0:T(8,128)S(1)}, f32[8,128]{1,0:T(8,128)S(1)}, u32[]{:S(2)}, u32[]{:S(2)}) collective-permute-start(f32[8,128]{1,0:T(8,128)S(1)} %get-tuple-element.37.s0), channel_id=1, source_target_pairs={{0,1},{1,0},{2,3},{3,2},{4,5},{5,4},{6,7},{7,6},{8,9},{9,8},{10,11... | collective-permute-start | bytes 12296 | tf_op jit(solution)/shard_map/ppermute | solution.py:409
  29.3 2.4 %collective-permute-start.7 = (bf16[256,640]{1,0:T(8,128)(2,1)S(1)}, bf16[256,640]{1,0:T(8,128)(2,1)S(1)}, u32[]{:S(2)}, u32[]{:S(2)}) collective-permute-start(bf16[256,640]{1,0:T(8,128)(2,1)S(1)} %get-tuple-element.45), channel_id=1, source_target_pairs={{0,4},{4,0},{8,12},{12,8},{16,20},{20,16},{24,28},{28,24},{32,36},... | collective-permute-start | bytes 983048 | tf_op jit(solution)/shard_map/ppermute | solution.py:398
  29.8 3.5 %collective-permute-start.6 = (bf16[256,640]{1,0:T(8,128)(2,1)S(1)}, bf16[256,640]{1,0:T(8,128)(2,1)S(1)}, u32[]{:S(2)}, u32[]{:S(2)}) collective-permute-start(bf16[256,640]{1,0:T(8,128)(2,1)S(1)} %get-tuple-element.44), channel_id=1, source_target_pairs={{0,4},{4,0},{8,12},{12,8},{16,20},{20,16},{24,28},{28,24},{32,36},... | collective-permute-start | bytes 983048 | tf_op jit(solution)/shard_map/ppermute | solution.py:398
  29.9 10.9 %collective-permute-start.8 = (bf16[256,640]{1,0:T(8,128)(2,1)S(1)}, bf16[256,640]{1,0:T(8,128)(2,1)S(1)}, u32[]{:S(2)}, u32[]{:S(2)}) collective-permute-start(bf16[256,640]{1,0:T(8,128)(2,1)S(1)} %get-tuple-element.45), channel_id=1, source_target_pairs={{0,4},{4,8},{8,12},{12,16},{16,20},{20,24},{24,28},{28,32},{32,36}... | collective-permute-start | bytes 983048 | tf_op jit(solution)/shard_map/ppermute | solution.py:398
  30.4 17.5 %collective-permute-start.12 = (bf16[640,512]{1,0:T(8,128)(2,1)S(1)}, bf16[640,512]{1,0:T(8,128)(2,1)S(1)}, u32[]{:S(2)}, u32[]{:S(2)}) collective-permute-start(bf16[640,512]{1,0:T(8,128)(2,1)S(1)} %collective-permute-done.5.pair_value.values), channel_id=1, source_target_pairs={{0,4},{4,0},{8,12},{12,8},{16,20},{20,16},{24,28},{28,24},{32,36},... | collective-permute-start | bytes 1966088 | tf_op jit(solution)/shard_map/ppermute | solution.py:398
  31.6 12.7 %collective-permute-start.9 = (bf16[256,640]{1,0:T(8,128)(2,1)S(1)}, bf16[256,640]{1,0:T(8,128)(2,1)S(1)}, u32[]{:S(2)}, u32[]{:S(2)}) collective-permute-start(bf16[256,640]{1,0:T(8,128)(2,1)S(1)} %get-tuple-element.44), channel_id=1, source_target_pairs={{0,4},{4,8},{8,12},{12,16},{16,20},{20,24},{24,28},{28,32},{32,36}... | collective-permute-start | bytes 983048 | tf_op jit(solution)/shard_map/ppermute | solution.py:398
  31.7 16.2 %collective-permute-start.10 = (bf16[256,640]{1,0:T(8,128)(2,1)S(1)}, bf16[256,640]{1,0:T(8,128)(2,1)S(1)}, u32[]{:S(2)}, u32[]{:S(2)}) collective-permute-start(bf16[256,640]{1,0:T(8,128)(2,1)S(1)} %collective-permute-done.7.pair_key_1), channel_id=1, source_target_pairs={{0,4},{4,8},{8,12},{12,16},{16,20},{20,24},{24,28},{28,32},{32,36}... | collective-permute-start | bytes 983048 | tf_op jit(solution)/shard_map/ppermute | solution.py:398
  40.9 7.0 %collective-permute-start.11 = (bf16[256,640]{1,0:T(8,128)(2,1)S(1)}, bf16[256,640]{1,0:T(8,128)(2,1)S(1)}, u32[]{:S(2)}, u32[]{:S(2)}) collective-permute-start(bf16[256,640]{1,0:T(8,128)(2,1)S(1)} %collective-permute-done.8.near_keys), channel_id=1, source_target_pairs={{0,4},{4,0},{8,12},{12,8},{16,20},{20,16},{24,28},{28,24},{32,36},... | collective-permute-start | bytes 983048 | tf_op jit(solution)/shard_map/ppermute | solution.py:398

commit v2 on v1

--- a/solution.py
+++ b/solution.py
@@ -11,6 +11,7 @@
 WIN = 4
 EPSILON = 1e-06
 MIB = 2**20
+PADDING = 16
 EXP2_SCALE = HD ** (-0.5) * 1.4426950408889634
 
 HBM = pl.BlockSpec(memory_space=pltpu.HBM)
@@ -63,9 +64,8 @@
         )
         for c in range(4)
     ]
-    for copy in small[:2] + lat_copies + small[2:]:
+    for copy in lat_copies[:1] + small[:2] + lat_copies[1:] + small[2:]:
         copy.start()
-    bounds = (0, 256, 640)
     fetches = [
         pltpu.make_async_copy(src, dst, w_sem.at[i])
         for i, (src, dst) in enumerate(
@@ -81,35 +81,48 @@
 
     for copy in small[:2]:
         copy.wait()
-    for f in range(2):
-        chosen = lax.broadcasted_iota(jnp.int32, (table.shape[0], 1), 0) == levels[f]
-        row = jnp.sum(jnp.where(chosen, table[...].astype(jnp.float32), 0.0), axis=0, keepdims=True)
-        shift[f : f + 1, :] = row[:, :width]
-        scale[f : f + 1, :] = 1.0 + row[:, width:]
+    pick = lax.broadcasted_iota(jnp.int32, (8, 1), 0)
+    wanted = jnp.where(pick == 0, levels[0], levels[1])
+    chosen = lax.broadcasted_iota(jnp.int32, (8, table.shape[0]), 1) == wanted
+    rows = jnp.dot(
+        chosen.astype(jnp.float32).astype(jnp.bfloat16), table[...], preferred_element_type=jnp.float32
+    )
+    shift[...] = rows[0:2, :width]
+    scale[...] = 1.0 + rows[0:2, width:]
+
+    def shape_rows(f, start, count):
+        rows = slice(start, start + count)
+        x = lat[rows, :].astype(jnp.float32)
+        center = jnp.mean(x, axis=1, keepdims=True)
+        x = x - center
+        spread = jnp.mean(x * x, axis=1, keepdims=True)
+        x = x * lax.rsqrt(spread + EPSILON)
+        shaped[rows, :] = (x * scale[f : f + 1, :] + shift[f : f + 1, :]).astype(jnp.bfloat16)
+
+    def value_rows(f):
+        rows = slice(f * frame, (f + 1) * frame)
+        result = jnp.dot(shaped[rows, :], weights[...], preferred_element_type=jnp.float32)
+        turned = jnp.transpose(result).astype(jnp.bfloat16)
+        value_both[:, rows] = turned
+        if f == 1:
+            value_early[...] = turned
 
     group = 64
-    for c in range(4):
+    for c in range(2):
         lat_copies[c].wait()
-        if c >= 1:
-            fetches[c - 1].start()
-        f = c // 2
-        for start in range(c * half, (c + 1) * half, group):
-            rows = slice(start, start + group)
-            x = lat[rows, :].astype(jnp.float32)
-            center = jnp.mean(x, axis=1, keepdims=True)
-            x = x - center
-            spread = jnp.mean(x * x, axis=1, keepdims=True)
-            x = x * lax.rsqrt(spread + EPSILON)
-            shaped[rows, :] = (x * scale[f : f + 1, :] + shift[f : f + 1, :]).astype(jnp.bfloat16)
-
-    fetches[3].start()
+        fetches[c].start()
+        for j in range(c * half, (c + 1) * half, group):
+            shape_rows(0, j, group)
+    for c in range(2, 4):
+        lat_copies[c].wait()
+        fetches[c].start()
     fetches[4].start()
-    for i, (s, e) in enumerate(zip(bounds, bounds[1:])):
-        fetches[i].wait()
-        result = jnp.dot(shaped[...], weights[:, s:e], preferred_element_type=jnp.float32)
-        turned = jnp.transpose(result).astype(jnp.bfloat16)
-        value_both[s:e, :] = turned
-        value_early[s:e, :] = turned[:, frame:]
+    fetches[0].wait()
+    fetches[1].wait()
+    for j in range(frame, 2 * frame, group):
+        shape_rows(1, j, group)
+    value_rows(0)
+    value_rows(1)
     for copy in small[2:]:
         copy.wait()
     info[0] = reaches[0]
@@ -155,7 +168,7 @@
             pltpu.SemaphoreType.DMA((4,)),
             pltpu.SemaphoreType.DMA((5,)),
         ],
-        compiler_params=pltpu.CompilerParams(vmem_limit_bytes=18 * MIB),
+        compiler_params=pltpu.CompilerParams(vmem_limit_bytes=22 * MIB),
         cost_estimate=pl.CostEstimate(
             flops=2 * rows * width * cols, bytes_accessed=26_000_000, transcendentals=0
         ),
@@ -211,14 +224,17 @@
     return as_columns(lax.rsqrt((first + second + (third + fourth)) / total_cols + EPSILON))
 
 
-def key_kernel(total_cols, key, gain, s0, s1, s2, s3, all_out, early, late):
+def key_kernel(total_cols, key, gain, s0, s1, s2, s3, all_out, early, late, passed):
     factor = norm_factor((s0, s1, s2, s3), 0, total_cols)
-    half = late.shape[0]
+    half = early.shape[0]
     for c in range(0, key.shape[1], 128):
         normed = (key[:, c : c + 128] * factor * gain[0:1, c : c + 128]).astype(jnp.bfloat16)
         all_out[:, c : c + 128] = normed
-        late[:, c : c + 128] = normed[:half]
+        late[:half, c : c + 128] = normed[:half]
+        late[half:, c : c + 128] = normed[: 2 * PADDING]
         early[:, c : c + 128] = normed[half:]
+        passed[:half, c : c + 128] = normed[half:]
+        passed[half:, c : c + 128] = normed[-PADDING:]
 
 
 def normalise_key(key, gain, sums, total_cols):
@@ -229,10 +245,11 @@
         out_shape=(
             jax.ShapeDtypeStruct((rows, cols), bf16),
             jax.ShapeDtypeStruct((rows // 2, cols), bf16),
-            jax.ShapeDtypeStruct((rows // 2, cols), bf16),
+            jax.ShapeDtypeStruct((rows // 2 + 2 * PADDING, cols), bf16),
+            jax.ShapeDtypeStruct((rows // 2 + PADDING, cols), bf16),
         ),
         in_specs=[VMEM] * 6,
-        out_specs=(VMEM,) * 3,
+        out_specs=(VMEM,) * 4,
         compiler_params=pltpu.CompilerParams(vmem_limit_bytes=12 * MIB),
         cost_estimate=pl.CostEstimate(flops=2 * rows * cols, bytes_accessed=100_000, transcendentals=0),
         name="normalise_key",
@@ -262,8 +279,7 @@
 
 
 def local_kernel(
-    total_cols, info, query, gain, s0, s1, s2, s3, key, value, pair_key_0, pair_key_1, pair_value,
-    query_out, acc, peak, mass,
+    total_cols, info, query, gain, s0, s1, s2, s3, key, value, query_out, acc, peak, mass,
 ):
     factor = norm_factor((s0, s1, s2, s3), 4, total_cols)
     for c in range(0, query.shape[1], 128):
@@ -273,52 +289,48 @@
     frame = query.shape[0] // 2
     at = [pl.ds(0, frame), pl.ds(frame, frame)]
     for f in range(2):
-        parts = (acc.at[f], peak.at[f], mass.at[f])
-        q = query_out.at[at[f]]
-        attend_block(True, q, key.at[at[f]], value.at[:, at[f]], *parts)
-        if f == 1:
-
-            @pl.when(info[f] >= 1)
-            def _():
-                attend_block(False, q, key.at[at[0]], value.at[:, at[0]], *parts)
-
-        for g, k in ((0, pair_key_0), (1, pair_key_1)):
-
-            @pl.when(jnp.logical_and(info[2] == 1, info[f] >= f + 2 - g))
-            def _():
-                attend_block(False, q, k, pair_value.at[:, at[g]], *parts)
-
-
-def local_attention(info, query, gain, sums, key, value, pairs, total_cols):
+        attend_block(
+            True, query_out.at[at[f]], key.at[at[f]], value.at[:, at[f]],
+            acc.at[f], peak.at[f], mass.at[f],
+        )
+
+    @pl.when(info[1] >= 1)
+    def _():
+        attend_block(
+            False, query_out.at[at[1]], key.at[at[0]], value.at[:, at[0]],
+            acc.at[1], peak.at[1], mass.at[1],
+        )
+
+
+def local_attention(info, query, gain, sums, key, value, total_cols):
     rows, cols = query.shape
     f32 = jnp.float32
-    stats = jax.ShapeDtypeStruct((2, 8, rows // 2), f32)
     return pl.pallas_call(
         functools.partial(local_kernel, total_cols),
         out_shape=(
-            jax.ShapeDtypeStruct((rows, cols), jnp.bfloat16),
-            jax.ShapeDtypeStruct((2, cols, rows // 2), f32),
-            stats,
-            stats,
-        ),
-        in_specs=[SMEM] + [VMEM] * 11,
+            pltpu.VMEM((rows, cols), jnp.bfloat16),
+            pltpu.VMEM((2, cols, rows // 2), f32),
+            pltpu.VMEM((2, 8, rows // 2), f32),
+            pltpu.VMEM((2, 8, rows // 2), f32),
+        ),
+        in_specs=[SMEM] + [VMEM] * 8,
         out_specs=(VMEM,) * 4,
         compiler_params=pltpu.CompilerParams(vmem_limit_bytes=12 * MIB),
         cost_estimate=pl.CostEstimate(flops=3_000_000, bytes_accessed=100_000, transcendentals=0),
         name="local_attention",
-    )(info, query, gain, *sums, key, value, *pairs)
+    )(info, query, gain, *sums, key, value)
 
 
 def near_kernel(info, query, acc_in, peak_in, mass_in, mid_keys, near_keys, values, acc, peak, mass):
-    keys = (mid_keys, near_keys)
     frame = query.shape[0] // 2
+    keys = (mid_keys.at[pl.ds(0, frame)], near_keys)
     at = [pl.ds(0, frame), pl.ds(frame, frame)]
     acc[...] = acc_in[...]
     peak[...] = peak_in[...]
     mass[...] = mass_in[...]
     for f, reach, g in ((0, 1, 1), (0, 2, 0), (1, 2, 1), (1, 3, 0)):
 
-        @pl.when(jnp.logical_and(info[2] == 0, info[f] >= reach))
+        @pl.when(info[f] >= reach)
         def _():
             attend_block(
                 False, query.at[at[f]], keys[g], values.at[:, at[g]],
@@ -352,7 +364,7 @@
     peak[...] = peak_in[0]
     mass[...] = mass_in[0]
     for core, k, v in (
-        (0, far_keys, far_values),
+        (0, far_keys.at[at[0]], far_values),
         (1, relayed_keys, relayed_values.at[:, at[1]]),
     ):
 
@@ -390,21 +402,32 @@
     latents, noise_level, lookback, level_table, w_query, w_key, w_value, gain_query, gain_key
 ):
     devices = lax.axis_size("queue")
-    total_cols = w_query.shape[1] * lax.axis_size("tp")
+    members = lax.axis_size("tp")
+    total_cols = w_query.shape[1] * members
     along = [(i, (i + 1) % devices) for i in range(devices)]
     swap = [(i, i ^ 1) for i in range(devices)]
 
+    def facing(i, t):
+        if i in (0, devices - 1):
+            return i * members + (t ^ 1)
+        return (i + 1 if i % 2 else i - 1) * members + t
+
+    across = [(i * members + t, facing(i, t)) for i in range(devices) for t in range(members)]
+
     def move(x, pairs):
         return lax.ppermute(x, "queue", pairs)
 
+    def move_across(x):
+        return lax.ppermute(x, ("queue", "tp"), across)
+
     shaped, key_weights, mixed_weights, value, value_early, gain_query, gain_key, info = project_value(
-        noise_level, lookback, latents, level_table, w_query, w_key, w_value,
-        gain_query, gain_key,
+        noise_level, lookback, latents, level_table, w_query, w_key, w_value, gain_query, gain_key
     )
     info = pltpu.with_memory_space_constraint(info, pltpu.SMEM)
     near_value = move(value, along)
-    far_value = move(move(value_early, swap), along)
+    pair_value = move(value_early, swap)
     query, key, sums = project_query_key(shaped, key_weights, mixed_weights, w_query)
+    pair_value, sums = lax.optimization_barrier((pair_value, sums))
     sums = [sums] + [
         lax.ppermute(sums, "tp", pairs)
         for pairs in (
@@ -413,16 +436,17 @@
             [(0, 2), (2, 0), (1, 3), (3, 1)],
         )
     ]
-    key_normed, key_early, key_late = normalise_key(key, gain_key, sums, total_cols)
+    far_value = move(pair_value, along)
+    key_normed, key_early, key_late, key_passed = normalise_key(key, gain_key, sums, total_cols)
     key_normed, far_value, near_value = lax.optimization_barrier((key_normed, far_value, near_value))
     relayed_value = move(near_value, swap)
     near_key = move(key_early, along)
     mid_key = move(key_late, along)
-    pair_key_1 = move(key_early, swap)
-    pair_key_0 = move(key_late, swap)
-    far_key = move(pair_key_1, along)
+    pair_key = move(key_passed, swap)
+    far_key = move_across(pair_key)
+    key_normed, pair_key = lax.optimization_barrier((key_normed, pair_key))
     query_normed, acc, peak, mass = local_attention(
-        info, query, gain_query, sums, key_normed, value, (pair_key_0, pair_key_1, near_value), total_cols
+        info, query, gain_query, sums, key_normed, value, total_cols
     )
     near_key, acc = lax.optimization_barrier((near_key, acc))
     relayed_key = move(near_key, swap)

time: 49.1 us -> 47.1 us (0.959)
  the two profiles are of different devices: /device:TPU:0 before, /device:TPU:32 now
where the time goes in v2:
time: 47.1 us; the launch traced here: 46.2 us
  Pallas kernels  24.9 us (53%)
  starting transfers between devices  11.9 us (25%)
  waiting for transfers between devices  9.27 us (20%)
    pallas_call x1, Pallas kernels, project_value(): pl.pallas_call(value_kernel, out_shape=(pltpu.VMEM((rows, width), bf16),...  11 us
    pallas_call x1, Pallas kernels, project_query_key(): pl.pallas_call(query_key_kernel, out_shape=(pltpu.VMEM((rows, cols), f32)...  7.36 us
    ppermute x8, waiting for transfers between devices, move(): return lax.ppermute(x, 'queue', pairs)  4.86 us
    ppermute x3, starting transfers between devices, on_device(): lax.ppermute(sums, 'tp', pairs)  4.15 us
    ppermute x8, starting transfers between devices, move(): return lax.ppermute(x, 'queue', pairs)  4.02 us
    ppermute x1, starting transfers between devices, move_across(): return lax.ppermute(x, ('queue', 'tp'), across)  3.78 us
    ppermute x3, waiting for transfers between devices, on_device(): lax.ppermute(sums, 'tp', pairs)  3.69 us
    pallas_call x1, Pallas kernels, near_attention(): pl.pallas_call(near_kernel, out_shape=(jax.ShapeDtypeStruct((2, cols, row...  2.99 us
  transfers between devices with their start and end apart: 12, of which 5 were waited for; matrix products, arithmetic and copies ran while one was open for 0% of the time, Pallas kernels for 28%

profile of v2, /device:TPU:32, one launch (start us, length us, event | category | flops | bytes accessed | tf_op | source)
XLA Modules:
  0.0 46.2 jit_solution(35003143125381748)
XLA Ops:
  0.0 11.0 %project_value.1 = (bf16[512,5120]{1,0:T(8,128)(2,1)S(1)}, bf16[5120,512]{1,0:T(8,128)(2,1)S(1)}, bf16[5120,256]{1,0:T(8,128)(2,1)S(1)}, bf16[640,512]{1,0:T(8,1...) custom-call(s32[2]{0:T(128)} %noise_level.1, ...), custom_call_target="tpu_custom_call" | custom-call | flops 3355443200 | bytes 26000000 | tf_op jit(solution)/shard_map/project_value/pallas_call | solution.py:145
  11.0 0.1 collective-permute-start
  11.1 0.5 %collective-permute-start.5 = (bf16[640,512]{1,0:T(8,128)(2,1)S(1)}, bf16[640,512]{1,0:T(8,128)(2,1)S(1)}, u32[]{:S(2)}, u32[]{:S(2)}) collective-permute-start(bf16[640,512]{1,0:T(8,128)(2,1)S(1)} %get-tuple-element.48.value), channel_id=1, source_target_pairs={{0,4},{4,8},{8,12},{12,16},{16,20},{20,24},{24,28},{28,32},{32,36}... | collective-permute-start | bytes 1966088 | tf_op jit(solution)/shard_map/ppermute | solution.py:418
  11.6 7.4 %project_query_key.1 = (f32[512,640]{1,0:T(8,128)S(1)}, f32[512,640]{1,0:T(8,128)S(1)}, f32[8,128]{1,0:T(8,128)S(1)}) custom-call(bf16[512,5120]{1,0:T(8,128)(2,1)S(1)} %get-tuple-element.36.shaped, bf16[5120,512]{1,0:T(8,128)(2,1)S(1)} %get-tuple-element.37.key_weights, bf16[5120,256]{1,0:T(8,128)(2,1)S(1)} %get-tuple-element.38.mixed_weights, ...), custom_call_target="tpu_custom_call" | custom-call | flops 6710886400 | bytes 18000000 | tf_op jit(solution)/shard_map/project_query_key/pallas_call | solution.py:204
  19.0 0.0 collective-permute-done
  19.0 1.5 %collective-permute-start.4 = (bf16[640,256]{1,0:T(8,128)(2,1)S(1)}, bf16[640,256]{1,0:T(8,128)(2,1)S(1)}, u32[]{:S(2)}, u32[]{:S(2)}) collective-permute-start(bf16[640,256]{1,0:T(8,128)(2,1)S(1)} %collective-permute-done), channel_id=1, source_target_pairs={{0,4},{4,8},{8,12},{12,16},{16,20},{20,24},{24,28},{28,32},{32,36}... | collective-permute-start | bytes 983048 | tf_op jit(solution)/shard_map/ppermute | solution.py:418
  20.5 3.0 %collective-permute-start.3 = (f32[8,128]{1,0:T(8,128)S(1)}, f32[8,128]{1,0:T(8,128)S(1)}, u32[]{:S(2)}, u32[]{:S(2)}) collective-permute-start(f32[8,128]{1,0:T(8,128)S(1)} %get-tuple-element.43.s0), channel_id=1, source_target_pairs={{0,2},{2,0},{1,3},{3,1},{4,6},{6,4},{5,7},{7,5},{8,10},{10,8},{9,1... | collective-permute-start | bytes 12296 | tf_op jit(solution)/shard_map/ppermute | solution.py:432
  23.5 1.1 %collective-permute-start.2 = (f32[8,128]{1,0:T(8,128)S(1)}, f32[8,128]{1,0:T(8,128)S(1)}, u32[]{:S(2)}, u32[]{:S(2)}) collective-permute-start(f32[8,128]{1,0:T(8,128)S(1)} %get-tuple-element.43.s0), channel_id=1, source_target_pairs={{0,3},{3,0},{1,2},{2,1},{4,7},{7,4},{5,6},{6,5},{8,11},{11,8},{9,1... | collective-permute-start | bytes 12296 | tf_op jit(solution)/shard_map/ppermute | solution.py:432
  24.6 0.0 collective-permute-start.1
  24.6 1.0 %collective-permute-done.3.s3 = f32[8,128]{1,0:T(8,128)S(1)} collective-permute-done((f32[8,128]{1,0:T(8,128)S(1)}, f32[8,128]{1,0:T(8,128)S(1)}, u32[]{:S(2)}, u32[]{:S(2)}) %collective-permute-start.3) | collective-permute-done | bytes 4128 | tf_op jit(solution)/shard_map/ppermute | solution.py:432
  25.6 2.7 %collective-permute-done.2.s2 = f32[8,128]{1,0:T(8,128)S(1)} collective-permute-done((f32[8,128]{1,0:T(8,128)S(1)}, f32[8,128]{1,0:T(8,128)S(1)}, u32[]{:S(2)}, u32[]{:S(2)}) %collective-permute-start.2) | collective-permute-done | bytes 4128 | tf_op jit(solution)/shard_map/ppermute | solution.py:432
  28.3 0.0 collective-permute-done.1.s1
  28.3 0.3 normalise_key.1
  28.6 0.1 collective-permute-start.6
  28.7 0.5 %collective-permute-start.7 = (bf16[256,640]{1,0:T(8,128)(2,1)S(1)}, bf16[256,640]{1,0:T(8,128)(2,1)S(1)}, u32[]{:S(2)}, u32[]{:S(2)}) collective-permute-start(bf16[256,640]{1,0:T(8,128)(2,1)S(1)} %get-tuple-element.53), channel_id=1, source_target_pairs={{0,4},{4,8},{8,12},{12,16},{16,20},{20,24},{24,28},{28,32},{32,36}... | collective-permute-start | bytes 983048 | tf_op jit(solution)/shard_map/ppermute | solution.py:418
  29.2 0.0 collective-permute-done.4.far_values
  29.2 0.0 collective-permute-done.5.values
  29.2 1.3 %collective-permute-start.11 = (bf16[640,512]{1,0:T(8,128)(2,1)S(1)}, bf16[640,512]{1,0:T(8,128)(2,1)S(1)}, u32[]{:S(2)}, u32[]{:S(2)}) collective-permute-start(bf16[640,512]{1,0:T(8,128)(2,1)S(1)} %collective-permute-done.5.values), channel_id=1, source_target_pairs={{0,4},{4,0},{8,12},{12,8},{16,20},{20,16},{24,28},{28,24},{32,36},... | collective-permute-start | bytes 1966088 | tf_op jit(solution)/shard_map/ppermute | solution.py:418
  30.5 0.1 collective-permute-start.8
  30.6 0.0 collective-permute-done.6
  30.6 3.8 %collective-permute-start.9 = (bf16[272,640]{1,0:T(8,128)(2,1)S(1)}, bf16[272,640]{1,0:T(8,128)(2,1)S(1)}, u32[]{:S(2)}, u32[]{:S(2)}) collective-permute-start(bf16[272,640]{1,0:T(8,128)(2,1)S(1)} %collective-permute-done.6), channel_id=1, source_target_pairs={{0,1},{1,0},{2,3},{3,2},{4,8},{5,9},{6,10},{7,11},{8,4},{9,5},{10,... | collective-permute-start | bytes 1044488 | tf_op jit(solution)/shard_map/ppermute | solution.py:421
  34.4 2.1 %local_attention.1 = (bf16[512,640]{1,0:T(8,128)(2,1)S(1)}, f32[2,640,256]{2,1,0:T(8,128)S(1)}, f32[2,8,256]{2,1,0:T(8,128)S(1)}, f32[2,8,256]{2,1,0:T(8,128)S(1)}) custom-call(s32[3]{0:T(128)S(4)} %get-tuple-element.35.info, f32[512,640]{1,0:T(8,128)S(1)} %get-tuple-element.39.query, f32[1,640]{1,0:T(1,128)S(1)} %get-tuple-element.40.gain, ...), custom_call_target="tpu_custom_call" | custom-call | flops 3000000 | bytes 100000 | tf_op jit(solution)/shard_map/local_attention/pallas_call | solution.py:308
  36.5 0.9 %collective-permute-done.7.near_keys = bf16[256,640]{1,0:T(8,128)(2,1)S(1)} collective-permute-done((bf16[256,640]{1,0:T(8,128)(2,1)S(1)}, bf16[256,640]{1,0:T(8,128)(2,1)S(1)}, u32[]{:S(2)}, u32[]{:S(2)}) %collective-permute-start.7) | collective-permute-done | bytes 327712 | tf_op jit(solution)/shard_map/ppermute | solution.py:418
  37.4 0.0 collective-permute-start.10
  37.4 3.9 %collective-permute-done.8.mid_keys = bf16[288,640]{1,0:T(8,128)(2,1)S(1)} collective-permute-done((bf16[288,640]{1,0:T(8,128)(2,1)S(1)}, bf16[288,640]{1,0:T(8,128)(2,1)S(1)}, u32[]{:S(2)}, u32[]{:S(2)}) %collective-permute-start.8) | collective-permute-done | bytes 368672 | tf_op jit(solution)/shard_map/ppermute | solution.py:418
  41.4 3.0 %near_attention.1 = (f32[2,640,256]{2,1,0:T(8,128)S(1)}, f32[2,8,256]{2,1,0:T(8,128)S(1)}, f32[2,8,256]{2,1,0:T(8,128)S(1)}) custom-call(s32[3]{0:T(128)S(4)} %get-tuple-element.35.info, bf16[512,640]{1,0:T(8,128)(2,1)S(1)} %get-tuple-element.52.query, f32[2,640,256]{2,1,0:T(8,128)S(1)} %get-tuple-element.55.acc_in, ...), custom_call_target="tpu_custom_call" | custom-call | flops 1000000 | bytes 100000 | tf_op jit(solution)/shard_map/near_attention/pallas_call | solution.py:345
  44.3 0.0 collective-permute-done.10.relayed_keys
  44.4 0.7 %collective-permute-done.9.far_keys = bf16[272,640]{1,0:T(8,128)(2,1)S(1)} collective-permute-done((bf16[272,640]{1,0:T(8,128)(2,1)S(1)}, bf16[272,640]{1,0:T(8,128)(2,1)S(1)}, u32[]{:S(2)}, u32[]{:S(2)}) %collective-permute-start.9) | collective-permute-done | bytes 348192 | tf_op jit(solution)/shard_map/ppermute | solution.py:421
  45.1 0.0 collective-permute-done.11.relayed_values
  45.1 1.1 %far_attention.1 = bf16[512,640]{1,0:T(8,128)(2,1)} custom-call(s32[3]{0:T(128)S(4)} %get-tuple-element.35.info, bf16[512,640]{1,0:T(8,128)(2,1)S(1)} %get-tuple-element.52.query, f32[2,640,256]{2,1,0:T(8,128)S(1)} %get-tuple-element.61.acc_in, f32[2,8,256]{2,1,0:T(8,128)S(1)} %get-tuple-element.62.peak_in, f32[2,8,256]{2,1,0:T(8,128)S(1)} %get-tuple-element.63.mass_in, ...), custom_call_target="tpu_custom_call" | custom-call | flops 1000000 | bytes 100000 | tf_op jit(solution)/shard_map/far_attention/pallas_call | solution.py:389
Async XLA Ops:
  11.0 8.0 %collective-permute-start = (bf16[640,256]{1,0:T(8,128)(2,1)S(1)}, bf16[640,256]{1,0:T(8,128)(2,1)S(1)}, u32[]{:S(2)}, u32[]{:S(2)}) collective-permute-start(bf16[640,256]{1,0:T(8,128)(2,1)S(1)} %get-tuple-element.41), channel_id=1, source_target_pairs={{0,4},{4,0},{8,12},{12,8},{16,20},{20,16},{24,28},{28,24},{32,36},... | collective-permute-start | bytes 983048 | tf_op jit(solution)/shard_map/ppermute | solution.py:418
  11.1 18.1 %collective-permute-start.5 = (bf16[640,512]{1,0:T(8,128)(2,1)S(1)}, bf16[640,512]{1,0:T(8,128)(2,1)S(1)}, u32[]{:S(2)}, u32[]{:S(2)}) collective-permute-start(bf16[640,512]{1,0:T(8,128)(2,1)S(1)} %get-tuple-element.48.value), channel_id=1, source_target_pairs={{0,4},{4,8},{8,12},{12,16},{16,20},{20,24},{24,28},{28,32},{32,36}... | collective-permute-start | bytes 1966088 | tf_op jit(solution)/shard_map/ppermute | solution.py:418
  19.0 10.2 %collective-permute-start.4 = (bf16[640,256]{1,0:T(8,128)(2,1)S(1)}, bf16[640,256]{1,0:T(8,128)(2,1)S(1)}, u32[]{:S(2)}, u32[]{:S(2)}) collective-permute-start(bf16[640,256]{1,0:T(8,128)(2,1)S(1)} %collective-permute-done), channel_id=1, source_target_pairs={{0,4},{4,8},{8,12},{12,16},{16,20},{20,24},{24,28},{28,32},{32,36}... | collective-permute-start | bytes 983048 | tf_op jit(solution)/shard_map/ppermute | solution.py:418
  20.5 5.1 %collective-permute-start.3 = (f32[8,128]{1,0:T(8,128)S(1)}, f32[8,128]{1,0:T(8,128)S(1)}, u32[]{:S(2)}, u32[]{:S(2)}) collective-permute-start(f32[8,128]{1,0:T(8,128)S(1)} %get-tuple-element.43.s0), channel_id=1, source_target_pairs={{0,2},{2,0},{1,3},{3,1},{4,6},{6,4},{5,7},{7,5},{8,10},{10,8},{9,1... | collective-permute-start | bytes 12296 | tf_op jit(solution)/shard_map/ppermute | solution.py:432
  23.5 4.8 %collective-permute-start.2 = (f32[8,128]{1,0:T(8,128)S(1)}, f32[8,128]{1,0:T(8,128)S(1)}, u32[]{:S(2)}, u32[]{:S(2)}) collective-permute-start(f32[8,128]{1,0:T(8,128)S(1)} %get-tuple-element.43.s0), channel_id=1, source_target_pairs={{0,3},{3,0},{1,2},{2,1},{4,7},{7,4},{5,6},{6,5},{8,11},{11,8},{9,1... | collective-permute-start | bytes 12296 | tf_op jit(solution)/shard_map/ppermute | solution.py:432
  24.6 3.7 %collective-permute-start.1 = (f32[8,128]{1,0:T(8,128)S(1)}, f32[8,128]{1,0:T(8,128)S(1)}, u32[]{:S(2)}, u32[]{:S(2)}) collective-permute-start(f32[8,128]{1,0:T(8,128)S(1)} %get-tuple-element.43.s0), channel_id=1, source_target_pairs={{0,1},{1,0},{2,3},{3,2},{4,5},{5,4},{6,7},{7,6},{8,9},{9,8},{10,11... | collective-permute-start | bytes 12296 | tf_op jit(solution)/shard_map/ppermute | solution.py:432
  28.6 1.9 %collective-permute-start.6 = (bf16[272,640]{1,0:T(8,128)(2,1)S(1)}, bf16[272,640]{1,0:T(8,128)(2,1)S(1)}, u32[]{:S(2)}, u32[]{:S(2)}) collective-permute-start(bf16[272,640]{1,0:T(8,128)(2,1)S(1)} %get-tuple-element.50), channel_id=1, source_target_pairs={{0,4},{4,0},{8,12},{12,8},{16,20},{20,16},{24,28},{28,24},{32,36},... | collective-permute-start | bytes 1044488 | tf_op jit(solution)/shard_map/ppermute | solution.py:418
  28.7 8.7 %collective-permute-start.7 = (bf16[256,640]{1,0:T(8,128)(2,1)S(1)}, bf16[256,640]{1,0:T(8,128)(2,1)S(1)}, u32[]{:S(2)}, u32[]{:S(2)}) collective-permute-start(bf16[256,640]{1,0:T(8,128)(2,1)S(1)} %get-tuple-element.53), channel_id=1, source_target_pairs={{0,4},{4,8},{8,12},{12,16},{16,20},{20,24},{24,28},{28,32},{32,36}... | collective-permute-start | bytes 983048 | tf_op jit(solution)/shard_map/ppermute | solution.py:418
  29.2 15.9 %collective-permute-start.11 = (bf16[640,512]{1,0:T(8,128)(2,1)S(1)}, bf16[640,512]{1,0:T(8,128)(2,1)S(1)}, u32[]{:S(2)}, u32[]{:S(2)}) collective-permute-start(bf16[640,512]{1,0:T(8,128)(2,1)S(1)} %collective-permute-done.5.values), channel_id=1, source_target_pairs={{0,4},{4,0},{8,12},{12,8},{16,20},{20,16},{24,28},{28,24},{32,36},... | collective-permute-start | bytes 1966088 | tf_op jit(solution)/shard_map/ppermute | solution.py:418
  30.5 10.9 %collective-permute-start.8 = (bf16[288,640]{1,0:T(8,128)(2,1)S(1)}, bf16[288,640]{1,0:T(8,128)(2,1)S(1)}, u32[]{:S(2)}, u32[]{:S(2)}) collective-permute-start(bf16[288,640]{1,0:T(8,128)(2,1)S(1)} %get-tuple-element.58), channel_id=1, source_target_pairs={{0,4},{4,8},{8,12},{12,16},{16,20},{20,24},{24,28},{28,32},{32,36}... | collective-permute-start | bytes 1105928 | tf_op jit(solution)/shard_map/ppermute | solution.py:418
  30.6 14.5 %collective-permute-start.9 = (bf16[272,640]{1,0:T(8,128)(2,1)S(1)}, bf16[272,640]{1,0:T(8,128)(2,1)S(1)}, u32[]{:S(2)}, u32[]{:S(2)}) collective-permute-start(bf16[272,640]{1,0:T(8,128)(2,1)S(1)} %collective-permute-done.6), channel_id=1, source_target_pairs={{0,1},{1,0},{2,3},{3,2},{4,8},{5,9},{6,10},{7,11},{8,4},{9,5},{10,... | collective-permute-start | bytes 1044488 | tf_op jit(solution)/shard_map/ppermute | solution.py:421
  37.4 6.9 %collective-permute-start.10 = (bf16[256,640]{1,0:T(8,128)(2,1)S(1)}, bf16[256,640]{1,0:T(8,128)(2,1)S(1)}, u32[]{:S(2)}, u32[]{:S(2)}) collective-permute-start(bf16[256,640]{1,0:T(8,128)(2,1)S(1)} %collective-permute-done.7.near_keys), channel_id=1, source_target_pairs={{0,4},{4,0},{8,12},{12,8},{16,20},{20,16},{24,28},{28,24},{32,36},... | collective-permute-start | bytes 983048 | tf_op jit(solution)/shard_map/ppermute | solution.py:418

commit v3 on v2

--- a/solution.py
+++ b/solution.py
@@ -11,6 +11,7 @@
 WIN = 4
 EPSILON = 1e-06
 MIB = 2**20
+VALUE_PADDING = 80
 PADDING = 16
 EXP2_SCALE = HD ** (-0.5) * 1.4426950408889634
 
@@ -105,7 +106,8 @@
         turned = jnp.transpose(result).astype(jnp.bfloat16)
         value_both[:, rows] = turned
         if f == 1:
-            value_early[...] = turned
+            value_early[:cols, :] = turned
+            value_early[cols:, :] = turned[:VALUE_PADDING]
 
     group = 64
     for c in range(2):
@@ -149,7 +151,7 @@
             pltpu.VMEM((width, main), bf16),
             pltpu.VMEM((width, 2 * (cols - main)), bf16),
             pltpu.VMEM((cols, rows), bf16),
-            pltpu.VMEM((cols, half), bf16),
+            pltpu.VMEM((cols + VALUE_PADDING, half), bf16),
             pltpu.VMEM((1, cols), f32),
             pltpu.VMEM((1, cols), f32),
             pltpu.SMEM((3,), jnp.int32),
@@ -321,36 +323,36 @@
     )(info, query, gain, *sums, key, value)
 
 
-def near_kernel(info, query, acc_in, peak_in, mass_in, mid_keys, near_keys, values, acc, peak, mass):
+def near_kernel(g, info, query, acc_in, peak_in, mass_in, keys, values, acc, peak, mass):
     frame = query.shape[0] // 2
-    keys = (mid_keys.at[pl.ds(0, frame)], near_keys)
     at = [pl.ds(0, frame), pl.ds(frame, frame)]
-    acc[...] = acc_in[...]
-    peak[...] = peak_in[...]
-    mass[...] = mass_in[...]
-    for f, reach, g in ((0, 1, 1), (0, 2, 0), (1, 2, 1), (1, 3, 0)):
-
-        @pl.when(info[f] >= reach)
+    for f in range(2):
+
+        @pl.when(info[f] >= f + 2 - g)
         def _():
             attend_block(
-                False, query.at[at[f]], keys[g], values.at[:, at[g]],
+                False, query.at[at[f]], keys.at[at[0]], values.at[:, at[g]],
                 acc.at[f], peak.at[f], mass.at[f],
             )
 
 
-def near_attention(info, query, acc, peak, mass, mid_keys, near_keys, values):
+def near_attention(g, info, query, acc, peak, mass, keys, values):
     rows, cols = query.shape
     f32 = jnp.float32
-    stats = jax.ShapeDtypeStruct((2, 8, rows // 2), f32)
-    return pl.pallas_call(
-        near_kernel,
-        out_shape=(jax.ShapeDtypeStruct((2, cols, rows // 2), f32), stats, stats),
-        in_specs=[SMEM] + [VMEM] * 7,
+    return pl.pallas_call(
+        functools.partial(near_kernel, g),
+        out_shape=(
+            pltpu.VMEM((2, cols, rows // 2), f32),
+            pltpu.VMEM((2, 8, rows // 2), f32),
+            pltpu.VMEM((2, 8, rows // 2), f32),
+        ),
+        in_specs=[SMEM] + [VMEM] * 6,
         out_specs=(VMEM,) * 3,
+        input_output_aliases={2: 0, 3: 1, 4: 2},
         compiler_params=pltpu.CompilerParams(vmem_limit_bytes=12 * MIB),
         cost_estimate=pl.CostEstimate(flops=1_000_000, bytes_accessed=100_000, transcendentals=0),
         name="near_attention",
-    )(info, query, acc, peak, mass, mid_keys, near_keys, values)
+    )(info, query, acc, peak, mass, keys, values)
 
 
 def far_kernel(
@@ -438,7 +440,7 @@
     ]
     far_value = move(pair_value, along)
     key_normed, key_early, key_late, key_passed = normalise_key(key, gain_key, sums, total_cols)
-    key_normed, far_value, near_value = lax.optimization_barrier((key_normed, far_value, near_value))
+    key_normed, near_value = lax.optimization_barrier((key_normed, near_value))
     relayed_value = move(near_value, swap)
     near_key = move(key_early, along)
     mid_key = move(key_late, along)
@@ -448,9 +450,10 @@
     query_normed, acc, peak, mass = local_attention(
         info, query, gain_query, sums, key_normed, value, total_cols
     )
-    near_key, acc = lax.optimization_barrier((near_key, acc))
+    near_key, acc, far_value = lax.optimization_barrier((near_key, acc, far_value))
     relayed_key = move(near_key, swap)
-    acc, peak, mass = near_attention(info, query_normed, acc, peak, mass, mid_key, near_key, near_value)
+    acc, peak, mass = near_attention(1, info, query_normed, acc, peak, mass, near_key, near_value)
+    acc, peak, mass = near_attention(0, info, query_normed, acc, peak, mass, mid_key, near_value)
     return far_attention(
         info, query_normed, acc, peak, mass, (far_key, far_value, relayed_key, relayed_value)
     )

time: 47.1 us -> 45.9 us (0.975)
  the two profiles are of different devices: /device:TPU:32 before, /device:TPU:66 now
where the time goes in v3:
time: 45.9 us; the launch traced here: 45.8 us
  Pallas kernels  24.8 us (54%)
  starting transfers between devices  11.7 us (25%)
  waiting for transfers between devices  9.21 us (20%)
    pallas_call x1, Pallas kernels, project_value(): pl.pallas_call(value_kernel, out_shape=(pltpu.VMEM((rows, width), bf16),...  11 us
    pallas_call x1, Pallas kernels, project_query_key(): pl.pallas_call(query_key_kernel, out_shape=(pltpu.VMEM((rows, cols), f32)...  7.3 us
    ppermute x8, waiting for transfers between devices, move(): return lax.ppermute(x, 'queue', pairs)  5.25 us
    ppermute x3, starting transfers between devices, on_device(): lax.ppermute(sums, 'tp', pairs)  4.78 us
    ppermute x1, starting transfers between devices, move_across(): return lax.ppermute(x, ('queue', 'tp'), across)  3.85 us
    ppermute x8, starting transfers between devices, move(): return lax.ppermute(x, 'queue', pairs)  3.08 us
    ppermute x1, waiting for transfers between devices, move_across(): return lax.ppermute(x, ('queue', 'tp'), across)  2.98 us
    pallas_call x2, Pallas kernels, near_attention(): pl.pallas_call(functools.partial(near_kernel, g), out_shape=(pltpu.VMEM((...  2.18 us
  transfers between devices with their start and end apart: 12, of which 5 were waited for; matrix products, arithmetic and copies ran while one was open for 0% of the time, Pallas kernels for 26%

profile of v3, /device:TPU:66, one launch (start us, length us, event | category | flops | bytes accessed | tf_op | source)
XLA Modules:
  0.0 45.8 jit_solution(7447089332461372288)
XLA Ops:
  0.0 11.0 %project_value.1 = (bf16[512,5120]{1,0:T(8,128)(2,1)S(1)}, bf16[5120,512]{1,0:T(8,128)(2,1)S(1)}, bf16[5120,256]{1,0:T(8,128)(2,1)S(1)}, bf16[640,512]{1,0:T(8,1...) custom-call(s32[2]{0:T(128)} %noise_level.1, ...), custom_call_target="tpu_custom_call" | custom-call | flops 3355443200 | bytes 26000000 | tf_op jit(solution)/shard_map/project_value/pallas_call | solution.py:147
  11.0 0.1 collective-permute-start
  11.1 0.5 %collective-permute-start.4 = (bf16[640,512]{1,0:T(8,128)(2,1)S(1)}, bf16[640,512]{1,0:T(8,128)(2,1)S(1)}, u32[]{:S(2)}, u32[]{:S(2)}) collective-permute-start(bf16[640,512]{1,0:T(8,128)(2,1)S(1)} %get-tuple-element.50.value), channel_id=1, source_target_pairs={{0,4},{4,8},{8,12},{12,16},{16,20},{20,24},{24,28},{28,32},{32,36}... | collective-permute-start | bytes 1966088 | tf_op jit(solution)/shard_map/ppermute | solution.py:420
  11.6 7.3 %project_query_key.1 = (f32[512,640]{1,0:T(8,128)S(1)}, f32[512,640]{1,0:T(8,128)S(1)}, f32[8,128]{1,0:T(8,128)S(1)}) custom-call(bf16[512,5120]{1,0:T(8,128)(2,1)S(1)} %get-tuple-element.39.shaped, bf16[5120,512]{1,0:T(8,128)(2,1)S(1)} %get-tuple-element.40.key_weights, bf16[5120,256]{1,0:T(8,128)(2,1)S(1)} %get-tuple-element.41.mixed_weights, ...), custom_call_target="tpu_custom_call" | custom-call | flops 6710886400 | bytes 18000000 | tf_op jit(solution)/shard_map/project_query_key/pallas_call | solution.py:206
  18.9 0.0 collective-permute-done
  18.9 2.2 %collective-permute-start.3 = (f32[8,128]{1,0:T(8,128)S(1)}, f32[8,128]{1,0:T(8,128)S(1)}, u32[]{:S(2)}, u32[]{:S(2)}) collective-permute-start(f32[8,128]{1,0:T(8,128)S(1)} %get-tuple-element.46.s0), channel_id=1, source_target_pairs={{0,2},{2,0},{1,3},{3,1},{4,6},{6,4},{5,7},{7,5},{8,10},{10,8},{9,1... | collective-permute-start | bytes 12296 | tf_op jit(solution)/shard_map/ppermute | solution.py:434
  21.1 0.0 collective-permute-start.2
  21.1 2.6 %collective-permute-start.1 = (f32[8,128]{1,0:T(8,128)S(1)}, f32[8,128]{1,0:T(8,128)S(1)}, u32[]{:S(2)}, u32[]{:S(2)}) collective-permute-start(f32[8,128]{1,0:T(8,128)S(1)} %get-tuple-element.46.s0), channel_id=1, source_target_pairs={{0,1},{1,0},{2,3},{3,2},{4,5},{5,4},{6,7},{7,6},{8,9},{9,8},{10,11... | collective-permute-start | bytes 12296 | tf_op jit(solution)/shard_map/ppermute | solution.py:434
  23.7 0.6 %collective-permute-start.7 = (bf16[720,256]{1,0:T(8,128)(2,1)S(1)}, bf16[720,256]{1,0:T(8,128)(2,1)S(1)}, u32[]{:S(2)}, u32[]{:S(2)}) collective-permute-start(bf16[720,256]{1,0:T(8,128)(2,1)S(1)} %collective-permute-done), channel_id=1, source_target_pairs={{0,4},{4,8},{8,12},{12,16},{16,20},{20,24},{24,28},{28,32},{32,36}... | collective-permute-start | bytes 1105928 | tf_op jit(solution)/shard_map/ppermute | solution.py:420
  24.3 0.0 collective-permute-done.3.s3
  24.3 0.4 collective-permute-done.2.s2
  24.7 0.6 %collective-permute-done.1.s1 = f32[8,128]{1,0:T(8,128)S(1)} collective-permute-done((f32[8,128]{1,0:T(8,128)S(1)}, f32[8,128]{1,0:T(8,128)S(1)}, u32[]{:S(2)}, u32[]{:S(2)}) %collective-permute-start.1) | collective-permute-done | bytes 4128 | tf_op jit(solution)/shard_map/ppermute | solution.py:434
  25.2 0.3 normalise_key.1
  25.5 0.2 collective-permute-start.5
  25.8 0.4 collective-permute-start.6
  26.1 0.0 collective-permute-done.4.values
  26.1 1.3 %collective-permute-start.11 = (bf16[640,512]{1,0:T(8,128)(2,1)S(1)}, bf16[640,512]{1,0:T(8,128)(2,1)S(1)}, u32[]{:S(2)}, u32[]{:S(2)}) collective-permute-start(bf16[640,512]{1,0:T(8,128)(2,1)S(1)} %collective-permute-done.4.values), channel_id=1, source_target_pairs={{0,4},{4,0},{8,12},{12,8},{16,20},{20,16},{24,28},{28,24},{32,36},... | collective-permute-start | bytes 1966088 | tf_op jit(solution)/shard_map/ppermute | solution.py:420
  27.4 0.0 collective-permute-start.8
  27.4 0.0 collective-permute-done.5
  27.4 3.9 %collective-permute-start.9 = (bf16[272,640]{1,0:T(8,128)(2,1)S(1)}, bf16[272,640]{1,0:T(8,128)(2,1)S(1)}, u32[]{:S(2)}, u32[]{:S(2)}) collective-permute-start(bf16[272,640]{1,0:T(8,128)(2,1)S(1)} %collective-permute-done.5), channel_id=1, source_target_pairs={{0,1},{1,0},{2,3},{3,2},{4,8},{5,9},{6,10},{7,11},{8,4},{9,5},{10,... | collective-permute-start | bytes 1044488 | tf_op jit(solution)/shard_map/ppermute | solution.py:423
  31.3 2.2 %local_attention.1 = (bf16[512,640]{1,0:T(8,128)(2,1)S(1)}, f32[2,640,256]{2,1,0:T(8,128)S(1)}, f32[2,8,256]{2,1,0:T(8,128)S(1)}, f32[2,8,256]{2,1,0:T(8,128)S(1)}) custom-call(s32[3]{0:T(128)S(4)} %get-tuple-element.38.info, f32[512,640]{1,0:T(8,128)S(1)} %get-tuple-element.42.query, f32[1,640]{1,0:T(1,128)S(1)} %get-tuple-element.43.gain, ...), custom_call_target="tpu_custom_call" | custom-call | flops 3000000 | bytes 100000 | tf_op jit(solution)/shard_map/local_attention/pallas_call | solution.py:310
  33.5 2.7 %collective-permute-done.6.keys = bf16[256,640]{1,0:T(8,128)(2,1)S(1)} collective-permute-done((bf16[256,640]{1,0:T(8,128)(2,1)S(1)}, bf16[256,640]{1,0:T(8,128)(2,1)S(1)}, u32[]{:S(2)}, u32[]{:S(2)}) %collective-permute-start.6) | collective-permute-done | bytes 327712 | tf_op jit(solution)/shard_map/ppermute | solution.py:420
  36.2 0.0 collective-permute-done.7.far_values
  36.2 0.0 collective-permute-start.10
  36.2 1.5 %near_attention.2 = (f32[2,640,256]{2,1,0:T(8,128)S(1)}, f32[2,8,256]{2,1,0:T(8,128)S(1)}, f32[2,8,256]{2,1,0:T(8,128)S(1)}) custom-call(s32[3]{0:T(128)S(4)} %get-tuple-element.38.info, bf16[512,640]{1,0:T(8,128)(2,1)S(1)} %get-tuple-element.54.query, ...), custom_call_target="tpu_custom_call", output_to_operand_aliasing={{0}: (2, {}), {1}: (3, {}), {2}: (4, {})} | custom-call | flops 1000000 | bytes 100000 | tf_op jit(solution)/shard_map/near_attention/pallas_call | solution.py:342
  37.7 2.5 %collective-permute-done.8.keys = bf16[288,640]{1,0:T(8,128)(2,1)S(1)} collective-permute-done((bf16[288,640]{1,0:T(8,128)(2,1)S(1)}, bf16[288,640]{1,0:T(8,128)(2,1)S(1)}, u32[]{:S(2)}, u32[]{:S(2)}) %collective-permute-start.8) | collective-permute-done | bytes 368672 | tf_op jit(solution)/shard_map/ppermute | solution.py:420
  40.2 0.7 %near_attention.3 = (f32[2,640,256]{2,1,0:T(8,128)S(1)}, f32[2,8,256]{2,1,0:T(8,128)S(1)}, f32[2,8,256]{2,1,0:T(8,128)S(1)}) custom-call(s32[3]{0:T(128)S(4)} %get-tuple-element.38.info, bf16[512,640]{1,0:T(8,128)(2,1)S(1)} %get-tuple-element.54.query, ...), custom_call_target="tpu_custom_call", output_to_operand_aliasing={{0}: (2, {}), {1}: (3, {}), {2}: (4, {})} | custom-call | flops 1000000 | bytes 100000 | tf_op jit(solution)/shard_map/near_attention/pallas_call | solution.py:342
  40.9 0.0 collective-permute-done.10.relayed_keys
  40.9 3.0 %collective-permute-done.9.far_keys = bf16[272,640]{1,0:T(8,128)(2,1)S(1)} collective-permute-done((bf16[272,640]{1,0:T(8,128)(2,1)S(1)}, bf16[272,640]{1,0:T(8,128)(2,1)S(1)}, u32[]{:S(2)}, u32[]{:S(2)}) %collective-permute-start.9) | collective-permute-done | bytes 348192 | tf_op jit(solution)/shard_map/ppermute | solution.py:423
  43.9 0.0 collective-permute-done.11.relayed_values
  43.9 1.9 %far_attention.1 = bf16[512,640]{1,0:T(8,128)(2,1)} custom-call(s32[3]{0:T(128)S(4)} %get-tuple-element.38.info, bf16[512,640]{1,0:T(8,128)(2,1)S(1)} %get-tuple-element.54.query, f32[2,640,256]{2,1,0:T(8,128)S(1)} %get-tuple-element.67.acc_in, f32[2,8,256]{2,1,0:T(8,128)S(1)} %get-tuple-element.68.peak_in, f32[2,8,256]{2,1,0:T(8,128)S(1)} %get-tuple-element.69.mass_in, ...), custom_call_target="tpu_custom_call" | custom-call | flops 1000000 | bytes 100000 | tf_op jit(solution)/shard_map/far_attention/pallas_call | solution.py:391
Async XLA Ops:
  11.0 7.9 %collective-permute-start = (bf16[720,256]{1,0:T(8,128)(2,1)S(1)}, bf16[720,256]{1,0:T(8,128)(2,1)S(1)}, u32[]{:S(2)}, u32[]{:S(2)}) collective-permute-start(bf16[720,256]{1,0:T(8,128)(2,1)S(1)} %get-tuple-element.44), channel_id=1, source_target_pairs={{0,4},{4,0},{8,12},{12,8},{16,20},{20,16},{24,28},{28,24},{32,36},... | collective-permute-start | bytes 1105928 | tf_op jit(solution)/shard_map/ppermute | solution.py:420
  11.1 15.1 %collective-permute-start.4 = (bf16[640,512]{1,0:T(8,128)(2,1)S(1)}, bf16[640,512]{1,0:T(8,128)(2,1)S(1)}, u32[]{:S(2)}, u32[]{:S(2)}) collective-permute-start(bf16[640,512]{1,0:T(8,128)(2,1)S(1)} %get-tuple-element.50.value), channel_id=1, source_target_pairs={{0,4},{4,8},{8,12},{12,16},{16,20},{20,24},{24,28},{28,32},{32,36}... | collective-permute-start | bytes 1966088 | tf_op jit(solution)/shard_map/ppermute | solution.py:420
  18.9 5.4 %collective-permute-start.3 = (f32[8,128]{1,0:T(8,128)S(1)}, f32[8,128]{1,0:T(8,128)S(1)}, u32[]{:S(2)}, u32[]{:S(2)}) collective-permute-start(f32[8,128]{1,0:T(8,128)S(1)} %get-tuple-element.46.s0), channel_id=1, source_target_pairs={{0,2},{2,0},{1,3},{3,1},{4,6},{6,4},{5,7},{7,5},{8,10},{10,8},{9,1... | collective-permute-start | bytes 12296 | tf_op jit(solution)/shard_map/ppermute | solution.py:434
  21.1 3.6 %collective-permute-start.2 = (f32[8,128]{1,0:T(8,128)S(1)}, f32[8,128]{1,0:T(8,128)S(1)}, u32[]{:S(2)}, u32[]{:S(2)}) collective-permute-start(f32[8,128]{1,0:T(8,128)S(1)} %get-tuple-element.46.s0), channel_id=1, source_target_pairs={{0,3},{3,0},{1,2},{2,1},{4,7},{7,4},{5,6},{6,5},{8,11},{11,8},{9,1... | collective-permute-start | bytes 12296 | tf_op jit(solution)/shard_map/ppermute | solution.py:434
  21.1 4.2 %collective-permute-start.1 = (f32[8,128]{1,0:T(8,128)S(1)}, f32[8,128]{1,0:T(8,128)S(1)}, u32[]{:S(2)}, u32[]{:S(2)}) collective-permute-start(f32[8,128]{1,0:T(8,128)S(1)} %get-tuple-element.46.s0), channel_id=1, source_target_pairs={{0,1},{1,0},{2,3},{3,2},{4,5},{5,4},{6,7},{7,6},{8,9},{9,8},{10,11... | collective-permute-start | bytes 12296 | tf_op jit(solution)/shard_map/ppermute | solution.py:434
  23.7 12.6 %collective-permute-start.7 = (bf16[720,256]{1,0:T(8,128)(2,1)S(1)}, bf16[720,256]{1,0:T(8,128)(2,1)S(1)}, u32[]{:S(2)}, u32[]{:S(2)}) collective-permute-start(bf16[720,256]{1,0:T(8,128)(2,1)S(1)} %collective-permute-done), channel_id=1, source_target_pairs={{0,4},{4,8},{8,12},{12,16},{16,20},{20,24},{24,28},{28,32},{32,36}... | collective-permute-start | bytes 1105928 | tf_op jit(solution)/shard_map/ppermute | solution.py:420
  25.5 1.9 %collective-permute-start.5 = (bf16[272,640]{1,0:T(8,128)(2,1)S(1)}, bf16[272,640]{1,0:T(8,128)(2,1)S(1)}, u32[]{:S(2)}, u32[]{:S(2)}) collective-permute-start(bf16[272,640]{1,0:T(8,128)(2,1)S(1)} %get-tuple-element.52), channel_id=1, source_target_pairs={{0,4},{4,0},{8,12},{12,8},{16,20},{20,16},{24,28},{28,24},{32,36},... | collective-permute-start | bytes 1044488 | tf_op jit(solution)/shard_map/ppermute | solution.py:420
  25.8 10.5 %collective-permute-start.6 = (bf16[256,640]{1,0:T(8,128)(2,1)S(1)}, bf16[256,640]{1,0:T(8,128)(2,1)S(1)}, u32[]{:S(2)}, u32[]{:S(2)}) collective-permute-start(bf16[256,640]{1,0:T(8,128)(2,1)S(1)} %get-tuple-element.55), channel_id=1, source_target_pairs={{0,4},{4,8},{8,12},{12,16},{16,20},{20,24},{24,28},{28,32},{32,36}... | collective-permute-start | bytes 983048 | tf_op jit(solution)/shard_map/ppermute | solution.py:420
  26.1 17.8 %collective-permute-start.11 = (bf16[640,512]{1,0:T(8,128)(2,1)S(1)}, bf16[640,512]{1,0:T(8,128)(2,1)S(1)}, u32[]{:S(2)}, u32[]{:S(2)}) collective-permute-start(bf16[640,512]{1,0:T(8,128)(2,1)S(1)} %collective-permute-done.4.values), channel_id=1, source_target_pairs={{0,4},{4,0},{8,12},{12,8},{16,20},{20,16},{24,28},{28,24},{32,36},... | collective-permute-start | bytes 1966088 | tf_op jit(solution)/shard_map/ppermute | solution.py:420
  27.4 12.7 %collective-permute-start.8 = (bf16[288,640]{1,0:T(8,128)(2,1)S(1)}, bf16[288,640]{1,0:T(8,128)(2,1)S(1)}, u32[]{:S(2)}, u32[]{:S(2)}) collective-permute-start(bf16[288,640]{1,0:T(8,128)(2,1)S(1)} %get-tuple-element.66), channel_id=1, source_target_pairs={{0,4},{4,8},{8,12},{12,16},{16,20},{20,24},{24,28},{28,32},{32,36}... | collective-permute-start | bytes 1105928 | tf_op jit(solution)/shard_map/ppermute | solution.py:420
  27.4 16.4 %collective-permute-start.9 = (bf16[272,640]{1,0:T(8,128)(2,1)S(1)}, bf16[272,640]{1,0:T(8,128)(2,1)S(1)}, u32[]{:S(2)}, u32[]{:S(2)}) collective-permute-start(bf16[272,640]{1,0:T(8,128)(2,1)S(1)} %collective-permute-done.5), channel_id=1, source_target_pairs={{0,1},{1,0},{2,3},{3,2},{4,8},{5,9},{6,10},{7,11},{8,4},{9,5},{10,... | collective-permute-start | bytes 1044488 | tf_op jit(solution)/shard_map/ppermute | solution.py:423
  36.2 4.7 %collective-permute-start.10 = (bf16[256,640]{1,0:T(8,128)(2,1)S(1)}, bf16[256,640]{1,0:T(8,128)(2,1)S(1)}, u32[]{:S(2)}, u32[]{:S(2)}) collective-permute-start(bf16[256,640]{1,0:T(8,128)(2,1)S(1)} %collective-permute-done.6.keys), channel_id=1, source_target_pairs={{0,4},{4,0},{8,12},{12,8},{16,20},{20,16},{24,28},{28,24},{32,36},... | collective-permute-start | bytes 983048 | tf_op jit(solution)/shard_map/ppermute | solution.py:420

commit v4 on v3

--- a/solution.py
+++ b/solution.py
@@ -226,6 +226,23 @@
     return as_columns(lax.rsqrt((first + second + (third + fourth)) / total_cols + EPSILON))
 
 
+def later_kernel(value, out):
+    cols, frame = out.shape
+    out[...] = value[:cols, frame:]
+
+
+def later_frame(value, cols):
+    return pl.pallas_call(
+        later_kernel,
+        out_shape=pltpu.VMEM((cols, value.shape[1] // 2), jnp.bfloat16),
+        in_specs=[VMEM],
+        out_specs=VMEM,
+        compiler_params=pltpu.CompilerParams(vmem_limit_bytes=8 * MIB),
+        cost_estimate=pl.CostEstimate(flops=1000, bytes_accessed=1000, transcendentals=0),
+        name="later_frame",
+    )(value)
+
+
 def key_kernel(total_cols, key, gain, s0, s1, s2, s3, all_out, early, late, passed):
     factor = norm_factor((s0, s1, s2, s3), 0, total_cols)
     half = early.shape[0]
@@ -367,7 +384,7 @@
     mass[...] = mass_in[0]
     for core, k, v in (
         (0, far_keys.at[at[0]], far_values),
-        (1, relayed_keys, relayed_values.at[:, at[1]]),
+        (1, relayed_keys, relayed_values),
     ):
 
         @pl.when(jnp.logical_and(info[2] == core, info[0] >= 3))
@@ -441,7 +458,7 @@
     far_value = move(pair_value, along)
     key_normed, key_early, key_late, key_passed = normalise_key(key, gain_key, sums, total_cols)
     key_normed, near_value = lax.optimization_barrier((key_normed, near_value))
-    relayed_value = move(near_value, swap)
+    relayed_value = move(later_frame(near_value, key.shape[1]), swap)
     near_key = move(key_early, along)
     mid_key = move(key_late, along)
     pair_key = move(key_passed, swap)

time: 45.9 us -> 45.9 us (level)
  starting transfers between devices: 11.7 us -> 10.5 us
  waiting for transfers between devices: 9.21 us -> 10.4 us
    ppermute x1, starting transfers between devices: 3.85 us -> 2.56 us  [move_across(): return lax.ppermute(x, ('queue', 'tp'), across)]
    ppermute x8, waiting for transfers between devices: 5.25 us -> 6.44 us  [move(): return lax.ppermute(x, 'queue', pairs)]
where the time goes in v4:
time: 45.9 us; the launch traced here: 45.8 us
  Pallas kernels  24.8 us (54%)
  starting transfers between devices  10.5 us (23%)
  waiting for transfers between devices  10.4 us (23%)
    pallas_call x1, Pallas kernels, project_value(): pl.pallas_call(value_kernel, out_shape=(pltpu.VMEM((rows, width), bf16),...  11 us
    pallas_call x1, Pallas kernels, project_query_key(): pl.pallas_call(query_key_kernel, out_shape=(pltpu.VMEM((rows, cols), f32)...  7.3 us
    ppermute x8, waiting for transfers between devices, move(): return lax.ppermute(x, 'queue', pairs)  6.44 us
    ppermute x3, starting transfers between devices, on_device(): lax.ppermute(sums, 'tp', pairs)  4.78 us
    ppermute x8, starting transfers between devices, move(): return lax.ppermute(x, 'queue', pairs)  3.16 us
    ppermute x1, waiting for transfers between devices, move_across(): return lax.ppermute(x, ('queue', 'tp'), across)  2.98 us
    ppermute x1, starting transfers between devices, move_across(): return lax.ppermute(x, ('queue', 'tp'), across)  2.56 us
    pallas_call x2, Pallas kernels, near_attention(): pl.pallas_call(functools.partial(near_kernel, g), out_shape=(pltpu.VMEM((...  2.17 us
  transfers between devices with their start and end apart: 12, of which 5 were waited for; matrix products, arithmetic and copies ran while one was open for 0% of the time, Pallas kernels for 26%

profile of v4, /device:TPU:66, one launch (start us, length us, event | category | flops | bytes accessed | tf_op | source)
XLA Modules:
  0.0 45.8 jit_solution(15174466199080680537)
XLA Ops:
  0.0 11.0 %project_value.1 = (bf16[512,5120]{1,0:T(8,128)(2,1)S(1)}, bf16[5120,512]{1,0:T(8,128)(2,1)S(1)}, bf16[5120,256]{1,0:T(8,128)(2,1)S(1)}, bf16[640,512]{1,0:T(8,1...) custom-call(s32[2]{0:T(128)} %noise_level.1, ...), custom_call_target="tpu_custom_call" | custom-call | flops 3355443200 | bytes 26000000 | tf_op jit(solution)/shard_map/project_value/pallas_call | solution.py:147
  11.0 0.1 collective-permute-start
  11.1 0.5 %collective-permute-start.4 = (bf16[640,512]{1,0:T(8,128)(2,1)S(1)}, bf16[640,512]{1,0:T(8,128)(2,1)S(1)}, u32[]{:S(2)}, u32[]{:S(2)}) collective-permute-start(bf16[640,512]{1,0:T(8,128)(2,1)S(1)} %get-tuple-element.50.value), channel_id=1, source_target_pairs={{0,4},{4,8},{8,12},{12,16},{16,20},{20,24},{24,28},{28,32},{32,36}... | collective-permute-start | bytes 1966088 | tf_op jit(solution)/shard_map/ppermute | solution.py:437
  11.6 7.3 %project_query_key.1 = (f32[512,640]{1,0:T(8,128)S(1)}, f32[512,640]{1,0:T(8,128)S(1)}, f32[8,128]{1,0:T(8,128)S(1)}) custom-call(bf16[512,5120]{1,0:T(8,128)(2,1)S(1)} %get-tuple-element.39.shaped, bf16[5120,512]{1,0:T(8,128)(2,1)S(1)} %get-tuple-element.40.key_weights, bf16[5120,256]{1,0:T(8,128)(2,1)S(1)} %get-tuple-element.41.mixed_weights, ...), custom_call_target="tpu_custom_call" | custom-call | flops 6710886400 | bytes 18000000 | tf_op jit(solution)/shard_map/project_query_key/pallas_call | solution.py:206
  18.9 0.0 collective-permute-done
  18.9 2.2 %collective-permute-start.3 = (f32[8,128]{1,0:T(8,128)S(1)}, f32[8,128]{1,0:T(8,128)S(1)}, u32[]{:S(2)}, u32[]{:S(2)}) collective-permute-start(f32[8,128]{1,0:T(8,128)S(1)} %get-tuple-element.46.s0), channel_id=1, source_target_pairs={{0,2},{2,0},{1,3},{3,1},{4,6},{6,4},{5,7},{7,5},{8,10},{10,8},{9,1... | collective-permute-start | bytes 12296 | tf_op jit(solution)/shard_map/ppermute | solution.py:451
  21.1 0.0 collective-permute-start.2
  21.1 2.6 %collective-permute-start.1 = (f32[8,128]{1,0:T(8,128)S(1)}, f32[8,128]{1,0:T(8,128)S(1)}, u32[]{:S(2)}, u32[]{:S(2)}) collective-permute-start(f32[8,128]{1,0:T(8,128)S(1)} %get-tuple-element.46.s0), channel_id=1, source_target_pairs={{0,1},{1,0},{2,3},{3,2},{4,5},{5,4},{6,7},{7,6},{8,9},{9,8},{10,11... | collective-permute-start | bytes 12296 | tf_op jit(solution)/shard_map/ppermute | solution.py:451
  23.7 0.6 %collective-permute-start.7 = (bf16[720,256]{1,0:T(8,128)(2,1)S(1)}, bf16[720,256]{1,0:T(8,128)(2,1)S(1)}, u32[]{:S(2)}, u32[]{:S(2)}) collective-permute-start(bf16[720,256]{1,0:T(8,128)(2,1)S(1)} %collective-permute-done), channel_id=1, source_target_pairs={{0,4},{4,8},{8,12},{12,16},{16,20},{20,24},{24,28},{28,32},{32,36}... | collective-permute-start | bytes 1105928 | tf_op jit(solution)/shard_map/ppermute | solution.py:437
  24.3 0.0 collective-permute-done.3.s3
  24.3 0.4 collective-permute-done.2.s2
  24.7 0.6 %collective-permute-done.1.s1 = f32[8,128]{1,0:T(8,128)S(1)} collective-permute-done((f32[8,128]{1,0:T(8,128)S(1)}, f32[8,128]{1,0:T(8,128)S(1)}, u32[]{:S(2)}, u32[]{:S(2)}) %collective-permute-start.1) | collective-permute-done | bytes 4128 | tf_op jit(solution)/shard_map/ppermute | solution.py:451
  25.2 0.3 normalise_key.1
  25.5 0.2 collective-permute-start.5
  25.8 0.4 collective-permute-start.6
  26.1 1.3 %collective-permute-start.8 = (bf16[288,640]{1,0:T(8,128)(2,1)S(1)}, bf16[288,640]{1,0:T(8,128)(2,1)S(1)}, u32[]{:S(2)}, u32[]{:S(2)}) collective-permute-start(bf16[288,640]{1,0:T(8,128)(2,1)S(1)} %get-tuple-element.66), channel_id=1, source_target_pairs={{0,4},{4,8},{8,12},{12,16},{16,20},{20,24},{24,28},{28,32},{32,36}... | collective-permute-start | bytes 1105928 | tf_op jit(solution)/shard_map/ppermute | solution.py:437
  27.4 0.0 collective-permute-done.5
  27.4 2.6 %collective-permute-start.9 = (bf16[272,640]{1,0:T(8,128)(2,1)S(1)}, bf16[272,640]{1,0:T(8,128)(2,1)S(1)}, u32[]{:S(2)}, u32[]{:S(2)}) collective-permute-start(bf16[272,640]{1,0:T(8,128)(2,1)S(1)} %collective-permute-done.5), channel_id=1, source_target_pairs={{0,1},{1,0},{2,3},{3,2},{4,8},{5,9},{6,10},{7,11},{8,4},{9,5},{10,... | collective-permute-start | bytes 1044488 | tf_op jit(solution)/shard_map/ppermute | solution.py:440
  30.0 0.0 collective-permute-done.4.values.value
  30.0 0.1 collective-permute-start.11
  30.1 2.2 %local_attention.1 = (bf16[512,640]{1,0:T(8,128)(2,1)S(1)}, f32[2,640,256]{2,1,0:T(8,128)S(1)}, f32[2,8,256]{2,1,0:T(8,128)S(1)}, f32[2,8,256]{2,1,0:T(8,128)S(1)}) custom-call(s32[3]{0:T(128)S(4)} %get-tuple-element.38.info, f32[512,640]{1,0:T(8,128)S(1)} %get-tuple-element.42.query, f32[1,640]{1,0:T(1,128)S(1)} %get-tuple-element.43.gain, ...), custom_call_target="tpu_custom_call" | custom-call | flops 3000000 | bytes 100000 | tf_op jit(solution)/shard_map/local_attention/pallas_call | solution.py:327
  32.3 3.9 %collective-permute-done.6.keys = bf16[256,640]{1,0:T(8,128)(2,1)S(1)} collective-permute-done((bf16[256,640]{1,0:T(8,128)(2,1)S(1)}, bf16[256,640]{1,0:T(8,128)(2,1)S(1)}, u32[]{:S(2)}, u32[]{:S(2)}) %collective-permute-start.6) | collective-permute-done | bytes 327712 | tf_op jit(solution)/shard_map/ppermute | solution.py:437
  36.2 0.0 collective-permute-done.7.far_values
  36.2 0.0 collective-permute-start.10
  36.2 1.5 %near_attention.2 = (f32[2,640,256]{2,1,0:T(8,128)S(1)}, f32[2,8,256]{2,1,0:T(8,128)S(1)}, f32[2,8,256]{2,1,0:T(8,128)S(1)}) custom-call(s32[3]{0:T(128)S(4)} %get-tuple-element.38.info, bf16[512,640]{1,0:T(8,128)(2,1)S(1)} %get-tuple-element.54.query, ...), custom_call_target="tpu_custom_call", output_to_operand_aliasing={{0}: (2, {}), {1}: (3, {}), {2}: (4, {})} | custom-call | flops 1000000 | bytes 100000 | tf_op jit(solution)/shard_map/near_attention/pallas_call | solution.py:359
  37.7 2.5 %collective-permute-done.8.keys = bf16[288,640]{1,0:T(8,128)(2,1)S(1)} collective-permute-done((bf16[288,640]{1,0:T(8,128)(2,1)S(1)}, bf16[288,640]{1,0:T(8,128)(2,1)S(1)}, u32[]{:S(2)}, u32[]{:S(2)}) %collective-permute-start.8) | collective-permute-done | bytes 368672 | tf_op jit(solution)/shard_map/ppermute | solution.py:437
  40.2 0.7 %near_attention.3 = (f32[2,640,256]{2,1,0:T(8,128)S(1)}, f32[2,8,256]{2,1,0:T(8,128)S(1)}, f32[2,8,256]{2,1,0:T(8,128)S(1)}) custom-call(s32[3]{0:T(128)S(4)} %get-tuple-element.38.info, bf16[512,640]{1,0:T(8,128)(2,1)S(1)} %get-tuple-element.54.query, ...), custom_call_target="tpu_custom_call", output_to_operand_aliasing={{0}: (2, {}), {1}: (3, {}), {2}: (4, {})} | custom-call | flops 1000000 | bytes 100000 | tf_op jit(solution)/shard_map/near_attention/pallas_call | solution.py:359
  40.9 0.0 collective-permute-done.11.relayed_values
  40.9 0.0 collective-permute-done.10.relayed_keys
  40.9 3.0 %collective-permute-done.9.far_keys = bf16[272,640]{1,0:T(8,128)(2,1)S(1)} collective-permute-done((bf16[272,640]{1,0:T(8,128)(2,1)S(1)}, bf16[272,640]{1,0:T(8,128)(2,1)S(1)}, u32[]{:S(2)}, u32[]{:S(2)}) %collective-permute-start.9) | collective-permute-done | bytes 348192 | tf_op jit(solution)/shard_map/ppermute | solution.py:440
  43.9 1.9 %far_attention.1 = bf16[512,640]{1,0:T(8,128)(2,1)} custom-call(s32[3]{0:T(128)S(4)} %get-tuple-element.38.info, bf16[512,640]{1,0:T(8,128)(2,1)S(1)} %get-tuple-element.54.query, f32[2,640,256]{2,1,0:T(8,128)S(1)} %get-tuple-element.67.acc_in, f32[2,8,256]{2,1,0:T(8,128)S(1)} %get-tuple-element.68.peak_in, f32[2,8,256]{2,1,0:T(8,128)S(1)} %get-tuple-element.69.mass_in, ...), custom_call_target="tpu_custom_call" | custom-call | flops 1000000 | bytes 100000 | tf_op jit(solution)/shard_map/far_attention/pallas_call | solution.py:408
  (1 shorter events, 0.0 us)
Async XLA Ops:
  11.0 7.9 %collective-permute-start = (bf16[720,256]{1,0:T(8,128)(2,1)S(1)}, bf16[720,256]{1,0:T(8,128)(2,1)S(1)}, u32[]{:S(2)}, u32[]{:S(2)}) collective-permute-start(bf16[720,256]{1,0:T(8,128)(2,1)S(1)} %get-tuple-element.44), channel_id=1, source_target_pairs={{0,4},{4,0},{8,12},{12,8},{16,20},{20,16},{24,28},{28,24},{32,36},... | collective-permute-start | bytes 1105928 | tf_op jit(solution)/shard_map/ppermute | solution.py:437
  11.1 18.9 %collective-permute-start.4 = (bf16[640,512]{1,0:T(8,128)(2,1)S(1)}, bf16[640,512]{1,0:T(8,128)(2,1)S(1)}, u32[]{:S(2)}, u32[]{:S(2)}) collective-permute-start(bf16[640,512]{1,0:T(8,128)(2,1)S(1)} %get-tuple-element.50.value), channel_id=1, source_target_pairs={{0,4},{4,8},{8,12},{12,16},{16,20},{20,24},{24,28},{28,32},{32,36}... | collective-permute-start | bytes 1966088 | tf_op jit(solution)/shard_map/ppermute | solution.py:437
  18.9 5.4 %collective-permute-start.3 = (f32[8,128]{1,0:T(8,128)S(1)}, f32[8,128]{1,0:T(8,128)S(1)}, u32[]{:S(2)}, u32[]{:S(2)}) collective-permute-start(f32[8,128]{1,0:T(8,128)S(1)} %get-tuple-element.46.s0), channel_id=1, source_target_pairs={{0,2},{2,0},{1,3},{3,1},{4,6},{6,4},{5,7},{7,5},{8,10},{10,8},{9,1... | collective-permute-start | bytes 12296 | tf_op jit(solution)/shard_map/ppermute | solution.py:451
  21.1 3.6 %collective-permute-start.2 = (f32[8,128]{1,0:T(8,128)S(1)}, f32[8,128]{1,0:T(8,128)S(1)}, u32[]{:S(2)}, u32[]{:S(2)}) collective-permute-start(f32[8,128]{1,0:T(8,128)S(1)} %get-tuple-element.46.s0), channel_id=1, source_target_pairs={{0,3},{3,0},{1,2},{2,1},{4,7},{7,4},{5,6},{6,5},{8,11},{11,8},{9,1... | collective-permute-start | bytes 12296 | tf_op jit(solution)/shard_map/ppermute | solution.py:451
  21.1 4.2 %collective-permute-start.1 = (f32[8,128]{1,0:T(8,128)S(1)}, f32[8,128]{1,0:T(8,128)S(1)}, u32[]{:S(2)}, u32[]{:S(2)}) collective-permute-start(f32[8,128]{1,0:T(8,128)S(1)} %get-tuple-element.46.s0), channel_id=1, source_target_pairs={{0,1},{1,0},{2,3},{3,2},{4,5},{5,4},{6,7},{7,6},{8,9},{9,8},{10,11... | collective-permute-start | bytes 12296 | tf_op jit(solution)/shard_map/ppermute | solution.py:451
  23.7 12.6 %collective-permute-start.7 = (bf16[720,256]{1,0:T(8,128)(2,1)S(1)}, bf16[720,256]{1,0:T(8,128)(2,1)S(1)}, u32[]{:S(2)}, u32[]{:S(2)}) collective-permute-start(bf16[720,256]{1,0:T(8,128)(2,1)S(1)} %collective-permute-done), channel_id=1, source_target_pairs={{0,4},{4,8},{8,12},{12,16},{16,20},{20,24},{24,28},{28,32},{32,36}... | collective-permute-start | bytes 1105928 | tf_op jit(solution)/shard_map/ppermute | solution.py:437
  25.5 1.9 %collective-permute-start.5 = (bf16[272,640]{1,0:T(8,128)(2,1)S(1)}, bf16[272,640]{1,0:T(8,128)(2,1)S(1)}, u32[]{:S(2)}, u32[]{:S(2)}) collective-permute-start(bf16[272,640]{1,0:T(8,128)(2,1)S(1)} %get-tuple-element.52), channel_id=1, source_target_pairs={{0,4},{4,0},{8,12},{12,8},{16,20},{20,16},{24,28},{28,24},{32,36},... | collective-permute-start | bytes 1044488 | tf_op jit(solution)/shard_map/ppermute | solution.py:437
  25.8 10.5 %collective-permute-start.6 = (bf16[256,640]{1,0:T(8,128)(2,1)S(1)}, bf16[256,640]{1,0:T(8,128)(2,1)S(1)}, u32[]{:S(2)}, u32[]{:S(2)}) collective-permute-start(bf16[256,640]{1,0:T(8,128)(2,1)S(1)} %get-tuple-element.55), channel_id=1, source_target_pairs={{0,4},{4,8},{8,12},{12,16},{16,20},{20,24},{24,28},{28,32},{32,36}... | collective-permute-start | bytes 983048 | tf_op jit(solution)/shard_map/ppermute | solution.py:437
  26.1 14.0 %collective-permute-start.8 = (bf16[288,640]{1,0:T(8,128)(2,1)S(1)}, bf16[288,640]{1,0:T(8,128)(2,1)S(1)}, u32[]{:S(2)}, u32[]{:S(2)}) collective-permute-start(bf16[288,640]{1,0:T(8,128)(2,1)S(1)} %get-tuple-element.66), channel_id=1, source_target_pairs={{0,4},{4,8},{8,12},{12,16},{16,20},{20,24},{24,28},{28,32},{32,36}... | collective-permute-start | bytes 1105928 | tf_op jit(solution)/shard_map/ppermute | solution.py:437
  27.4 16.5 %collective-permute-start.9 = (bf16[272,640]{1,0:T(8,128)(2,1)S(1)}, bf16[272,640]{1,0:T(8,128)(2,1)S(1)}, u32[]{:S(2)}, u32[]{:S(2)}) collective-permute-start(bf16[272,640]{1,0:T(8,128)(2,1)S(1)} %collective-permute-done.5), channel_id=1, source_target_pairs={{0,1},{1,0},{2,3},{3,2},{4,8},{5,9},{6,10},{7,11},{8,4},{9,5},{10,... | collective-permute-start | bytes 1044488 | tf_op jit(solution)/shard_map/ppermute | solution.py:440
  30.0 10.9 %collective-permute-start.11 = (bf16[640,256]{1,0:T(8,128)(2,1)S(1)}, bf16[640,256]{1,0:T(8,128)(2,1)S(1)}, u32[]{:S(2)}, u32[]{:S(2)}) collective-permute-start(bf16[640,256]{1,0:T(8,128)(2,1)S(1)} %later_frame.1), channel_id=1, source_target_pairs={{0,4},{4,0},{8,12},{12,8},{16,20},{20,16},{24,28},{28,24},{32,36},... | collective-permute-start | bytes 983048 | tf_op jit(solution)/shard_map/ppermute | solution.py:437
  36.2 4.7 %collective-permute-start.10 = (bf16[256,640]{1,0:T(8,128)(2,1)S(1)}, bf16[256,640]{1,0:T(8,128)(2,1)S(1)}, u32[]{:S(2)}, u32[]{:S(2)}) collective-permute-start(bf16[256,640]{1,0:T(8,128)(2,1)S(1)} %collective-permute-done.6.keys), channel_id=1, source_target_pairs={{0,4},{4,0},{8,12},{12,8},{16,20},{20,16},{24,28},{28,24},{32,36},... | collective-permute-start | bytes 983048 | tf_op jit(solution)/shard_map/ppermute | solution.py:437

commit v5 on v4

--- a/solution.py
+++ b/solution.py
@@ -340,7 +340,13 @@
     )(info, query, gain, *sums, key, value)
 
 
-def near_kernel(g, info, query, acc_in, peak_in, mass_in, keys, values, acc, peak, mass):
+def finish(acc, mass, out):
+    for h in range(acc.shape[0] // HD):
+        c = slice(h * HD, (h + 1) * HD)
+        out[:, c] = jnp.transpose(acc[c, :] / mass[h : h + 1, :]).astype(out.dtype)
+
+
+def near_kernel(g, info, query, acc_in, peak_in, mass_in, keys, values, acc, peak, mass, *second):
     frame = query.shape[0] // 2
     at = [pl.ds(0, frame), pl.ds(frame, frame)]
     for f in range(2):
@@ -352,19 +358,24 @@
                 acc.at[f], peak.at[f], mass.at[f],
             )
 
+    for out in second:
+        finish(acc.at[1], mass.at[1], out)
+
 
 def near_attention(g, info, query, acc, peak, mass, keys, values):
     rows, cols = query.shape
     f32 = jnp.float32
+    second = (pltpu.VMEM((rows // 2, cols), jnp.bfloat16),) if g == 0 else ()
     return pl.pallas_call(
         functools.partial(near_kernel, g),
         out_shape=(
             pltpu.VMEM((2, cols, rows // 2), f32),
             pltpu.VMEM((2, 8, rows // 2), f32),
             pltpu.VMEM((2, 8, rows // 2), f32),
-        ),
+        )
+        + second,
         in_specs=[SMEM] + [VMEM] * 6,
-        out_specs=(VMEM,) * 3,
+        out_specs=(VMEM,) * (3 + len(second)),
         input_output_aliases={2: 0, 3: 1, 4: 2},
         compiler_params=pltpu.CompilerParams(vmem_limit_bytes=12 * MIB),
         cost_estimate=pl.CostEstimate(flops=1_000_000, bytes_accessed=100_000, transcendentals=0),
@@ -373,10 +384,9 @@
 
 
 def far_kernel(
-    info, query, acc_in, peak_in, mass_in, far_keys, far_values, relayed_keys, relayed_values,
+    info, query, acc_in, peak_in, mass_in, second, far_keys, far_values, relayed_keys, relayed_values,
     out, acc, peak, mass,
 ):
-    cols = query.shape[1]
     frame = query.shape[0] // 2
     at = [pl.ds(0, frame), pl.ds(frame, frame)]
     acc[...] = acc_in[0]
@@ -391,30 +401,24 @@
         def _():
             attend_block(False, query.at[at[0]], k, v, acc, peak, mass)
 
-    for f in range(2):
-        for h in range(cols // HD):
-            c = slice(h * HD, (h + 1) * HD)
-            if f == 0:
-                result = acc[c, :] / mass[h : h + 1, :]
-            else:
-                result = acc_in[f, c, :] / mass_in[f, h : h + 1, :]
-            out[at[f], c] = jnp.transpose(result).astype(out.dtype)
-
-
-def far_attention(info, query, acc, peak, mass, halo):
+    out[at[1], :] = second[...]
+    finish(acc, mass, out.at[at[0]])
+
+
+def far_attention(info, query, acc, peak, mass, second, halo):
     rows, cols = query.shape
     f32 = jnp.float32
     stats = pltpu.VMEM((8, rows // 2), f32)
     return pl.pallas_call(
         far_kernel,
         out_shape=jax.ShapeDtypeStruct((rows, cols), jnp.bfloat16),
-        in_specs=[SMEM] + [VMEM] * 8,
+        in_specs=[SMEM] + [VMEM] * 9,
         out_specs=VMEM,
         scratch_shapes=[pltpu.VMEM((cols, rows // 2), f32), stats, stats],
         compiler_params=pltpu.CompilerParams(vmem_limit_bytes=12 * MIB),
         cost_estimate=pl.CostEstimate(flops=1_000_000, bytes_accessed=100_000, transcendentals=0),
         name="far_attention",
-    )(info, query, acc, peak, mass, *halo)
+    )(info, query, acc, peak, mass, second, *halo)
 
 
 def on_device(
@@ -470,9 +474,11 @@
     near_key, acc, far_value = lax.optimization_barrier((near_key, acc, far_value))
     relayed_key = move(near_key, swap)
     acc, peak, mass = near_attention(1, info, query_normed, acc, peak, mass, near_key, near_value)
-    acc, peak, mass = near_attention(0, info, query_normed, acc, peak, mass, mid_key, near_value)
+    acc, peak, mass, second = near_attention(
+        0, info, query_normed, acc, peak, mass, mid_key, near_value
+    )
     return far_attention(
-        info, query_normed, acc, peak, mass, (far_key, far_value, relayed_key, relayed_value)
+        info, query_normed, acc, peak, mass, second, (far_key, far_value, relayed_key, relayed_value)
     )
 
 

time: 45.9 us -> 45.4 us (0.989)
  Pallas kernels: 24.8 us -> 23.4 us
  waiting for transfers between devices: 10.4 us -> 10.9 us
    pallas_call x1, Pallas kernels: 1.87 us -> 1.06 us  [far_attention(): pl.pallas_call(far_kernel, out_shape=jax.ShapeDtypeStruct((rows, cols), j...]
    ppermute x8, waiting for transfers between devices: 6.44 us -> 7.15 us  [move(): return lax.ppermute(x, 'queue', pairs)]
    pallas_call x2, Pallas kernels: 2.17 us -> 1.64 us  [near_attention(): pl.pallas_call(functools.partial(near_kernel, g), out_shape=(pltpu.VMEM((...]
  transfers between devices with their start and end apart: 12 -> 12, of which waited for: 5 -> 5; matrix products, arithmetic and copies ran while one was open for 0% -> 0% of each run, Pallas kernels for 26% -> 25%
where the time goes in v5:
time: 45.4 us; the launch traced here: 45 us
  Pallas kernels  23.4 us (52%)
  waiting for transfers between devices  10.9 us (24%)
  starting transfers between devices  10.5 us (23%)
    pallas_call x1, Pallas kernels, project_value(): pl.pallas_call(value_kernel, out_shape=(pltpu.VMEM((rows, width), bf16),...  11 us
    pallas_call x1, Pallas kernels, project_query_key(): pl.pallas_call(query_key_kernel, out_shape=(pltpu.VMEM((rows, cols), f32)...  7.3 us
    ppermute x8, waiting for transfers between devices, move(): return lax.ppermute(x, 'queue', pairs)  7.15 us
    ppermute x3, starting transfers between devices, on_device(): lax.ppermute(sums, 'tp', pairs)  4.78 us
    ppermute x8, starting transfers between devices, move(): return lax.ppermute(x, 'queue', pairs)  3.16 us
    ppermute x1, waiting for transfers between devices, move_across(): return lax.ppermute(x, ('queue', 'tp'), across)  2.8 us
    ppermute x1, starting transfers between devices, move_across(): return lax.ppermute(x, ('queue', 'tp'), across)  2.56 us
    pallas_call x1, Pallas kernels, local_attention(): pl.pallas_call(functools.partial(local_kernel, total_cols), out_shape=(pl...  2.16 us
  transfers between devices with their start and end apart: 12, of which 5 were waited for; matrix products, arithmetic and copies ran while one was open for 0% of the time, Pallas kernels for 25%

profile of v5, /device:TPU:66, one launch (start us, length us, event | category | flops | bytes accessed | tf_op | source)
XLA Modules:
  0.0 45.0 jit_solution(18393716697656374776)
XLA Ops:
  0.0 11.0 %project_value.1 = (bf16[512,5120]{1,0:T(8,128)(2,1)S(1)}, bf16[5120,512]{1,0:T(8,128)(2,1)S(1)}, bf16[5120,256]{1,0:T(8,128)(2,1)S(1)}, bf16[640,512]{1,0:T(8,1...) custom-call(s32[2]{0:T(128)} %noise_level.1, ...), custom_call_target="tpu_custom_call" | custom-call | flops 3355443200 | bytes 26000000 | tf_op jit(solution)/shard_map/project_value/pallas_call | solution.py:147
  11.0 0.1 collective-permute-start
  11.1 0.5 %collective-permute-start.4 = (bf16[640,512]{1,0:T(8,128)(2,1)S(1)}, bf16[640,512]{1,0:T(8,128)(2,1)S(1)}, u32[]{:S(2)}, u32[]{:S(2)}) collective-permute-start(bf16[640,512]{1,0:T(8,128)(2,1)S(1)} %get-tuple-element.51.value), channel_id=1, source_target_pairs={{0,4},{4,8},{8,12},{12,16},{16,20},{20,24},{24,28},{28,32},{32,36}... | collective-permute-start | bytes 1966088 | tf_op jit(solution)/shard_map/ppermute | solution.py:441
  11.6 7.3 %project_query_key.1 = (f32[512,640]{1,0:T(8,128)S(1)}, f32[512,640]{1,0:T(8,128)S(1)}, f32[8,128]{1,0:T(8,128)S(1)}) custom-call(bf16[512,5120]{1,0:T(8,128)(2,1)S(1)} %get-tuple-element.40.shaped, bf16[5120,512]{1,0:T(8,128)(2,1)S(1)} %get-tuple-element.41.key_weights, bf16[5120,256]{1,0:T(8,128)(2,1)S(1)} %get-tuple-element.42.mixed_weights, ...), custom_call_target="tpu_custom_call" | custom-call | flops 6710886400 | bytes 18000000 | tf_op jit(solution)/shard_map/project_query_key/pallas_call | solution.py:206
  18.9 0.0 collective-permute-done
  18.9 2.2 %collective-permute-start.3 = (f32[8,128]{1,0:T(8,128)S(1)}, f32[8,128]{1,0:T(8,128)S(1)}, u32[]{:S(2)}, u32[]{:S(2)}) collective-permute-start(f32[8,128]{1,0:T(8,128)S(1)} %get-tuple-element.47.s0), channel_id=1, source_target_pairs={{0,2},{2,0},{1,3},{3,1},{4,6},{6,4},{5,7},{7,5},{8,10},{10,8},{9,1... | collective-permute-start | bytes 12296 | tf_op jit(solution)/shard_map/ppermute | solution.py:455
  21.1 0.0 collective-permute-start.2
  21.1 2.6 %collective-permute-start.1 = (f32[8,128]{1,0:T(8,128)S(1)}, f32[8,128]{1,0:T(8,128)S(1)}, u32[]{:S(2)}, u32[]{:S(2)}) collective-permute-start(f32[8,128]{1,0:T(8,128)S(1)} %get-tuple-element.47.s0), channel_id=1, source_target_pairs={{0,1},{1,0},{2,3},{3,2},{4,5},{5,4},{6,7},{7,6},{8,9},{9,8},{10,11... | collective-permute-start | bytes 12296 | tf_op jit(solution)/shard_map/ppermute | solution.py:455
  23.7 0.6 %collective-permute-start.7 = (bf16[720,256]{1,0:T(8,128)(2,1)S(1)}, bf16[720,256]{1,0:T(8,128)(2,1)S(1)}, u32[]{:S(2)}, u32[]{:S(2)}) collective-permute-start(bf16[720,256]{1,0:T(8,128)(2,1)S(1)} %collective-permute-done), channel_id=1, source_target_pairs={{0,4},{4,8},{8,12},{12,16},{16,20},{20,24},{24,28},{28,32},{32,36}... | collective-permute-start | bytes 1105928 | tf_op jit(solution)/shard_map/ppermute | solution.py:441
  24.3 0.0 collective-permute-done.3.s3
  24.3 0.4 collective-permute-done.2.s2
  24.7 0.6 %collective-permute-done.1.s1 = f32[8,128]{1,0:T(8,128)S(1)} collective-permute-done((f32[8,128]{1,0:T(8,128)S(1)}, f32[8,128]{1,0:T(8,128)S(1)}, u32[]{:S(2)}, u32[]{:S(2)}) %collective-permute-start.1) | collective-permute-done | bytes 4128 | tf_op jit(solution)/shard_map/ppermute | solution.py:455
  25.2 0.3 normalise_key.1
  25.5 0.2 collective-permute-start.5
  25.8 0.4 collective-permute-start.6
  26.1 1.3 %collective-permute-start.8 = (bf16[288,640]{1,0:T(8,128)(2,1)S(1)}, bf16[288,640]{1,0:T(8,128)(2,1)S(1)}, u32[]{:S(2)}, u32[]{:S(2)}) collective-permute-start(bf16[288,640]{1,0:T(8,128)(2,1)S(1)} %get-tuple-element.67), channel_id=1, source_target_pairs={{0,4},{4,8},{8,12},{12,16},{16,20},{20,24},{24,28},{28,32},{32,36}... | collective-permute-start | bytes 1105928 | tf_op jit(solution)/shard_map/ppermute | solution.py:441
  27.4 0.0 collective-permute-done.5
  27.4 2.6 %collective-permute-start.9 = (bf16[272,640]{1,0:T(8,128)(2,1)S(1)}, bf16[272,640]{1,0:T(8,128)(2,1)S(1)}, u32[]{:S(2)}, u32[]{:S(2)}) collective-permute-start(bf16[272,640]{1,0:T(8,128)(2,1)S(1)} %collective-permute-done.5), channel_id=1, source_target_pairs={{0,1},{1,0},{2,3},{3,2},{4,8},{5,9},{6,10},{7,11},{8,4},{9,5},{10,... | collective-permute-start | bytes 1044488 | tf_op jit(solution)/shard_map/ppermute | solution.py:444
  30.0 0.0 collective-permute-done.4.values.value
  30.0 0.1 collective-permute-start.11
  30.1 2.2 %local_attention.1 = (bf16[512,640]{1,0:T(8,128)(2,1)S(1)}, f32[2,640,256]{2,1,0:T(8,128)S(1)}, f32[2,8,256]{2,1,0:T(8,128)S(1)}, f32[2,8,256]{2,1,0:T(8,128)S(1)}) custom-call(s32[3]{0:T(128)S(4)} %get-tuple-element.39.info, f32[512,640]{1,0:T(8,128)S(1)} %get-tuple-element.43.query, f32[1,640]{1,0:T(1,128)S(1)} %get-tuple-element.44.gain, ...), custom_call_target="tpu_custom_call" | custom-call | flops 3000000 | bytes 100000 | tf_op jit(solution)/shard_map/local_attention/pallas_call | solution.py:327
  32.3 3.9 %collective-permute-done.6.keys = bf16[256,640]{1,0:T(8,128)(2,1)S(1)} collective-permute-done((bf16[256,640]{1,0:T(8,128)(2,1)S(1)}, bf16[256,640]{1,0:T(8,128)(2,1)S(1)}, u32[]{:S(2)}, u32[]{:S(2)}) %collective-permute-start.6) | collective-permute-done | bytes 327712 | tf_op jit(solution)/shard_map/ppermute | solution.py:441
  36.2 0.0 collective-permute-done.7.far_values
  36.2 0.0 collective-permute-start.10
  36.2 0.7 %near_attention.2 = (f32[2,640,256]{2,1,0:T(8,128)S(1)}, f32[2,8,256]{2,1,0:T(8,128)S(1)}, f32[2,8,256]{2,1,0:T(8,128)S(1)}) custom-call(s32[3]{0:T(128)S(4)} %get-tuple-element.39.info, bf16[512,640]{1,0:T(8,128)(2,1)S(1)} %get-tuple-element.55.query, ...), custom_call_target="tpu_custom_call", output_to_operand_aliasing={{0}: (2, {}), {1}: (3, {}), {2}: (4, {})} | custom-call | flops 1000000 | bytes 100000 | tf_op jit(solution)/shard_map/near_attention/pallas_call | solution.py:369
  37.0 3.2 %collective-permute-done.8.keys = bf16[288,640]{1,0:T(8,128)(2,1)S(1)} collective-permute-done((bf16[288,640]{1,0:T(8,128)(2,1)S(1)}, bf16[288,640]{1,0:T(8,128)(2,1)S(1)}, u32[]{:S(2)}, u32[]{:S(2)}) %collective-permute-start.8) | collective-permute-done | bytes 368672 | tf_op jit(solution)/shard_map/ppermute | solution.py:441
  40.2 0.9 %near_attention.3 = (f32[2,640,256]{2,1,0:T(8,128)S(1)}, f32[2,8,256]{2,1,0:T(8,128)S(1)}, f32[2,8,256]{2,1,0:T(8,128)S(1)}, bf16[256,640]{1,0:T(8,128)(2,1)S(1)}) custom-call(s32[3]{0:T(128)S(4)} %get-tuple-element.39.info, bf16[512,640]{1,0:T(8,128)(2,1)S(1)} %get-tuple-element.55.query, ...), custom_call_target="tpu_custom_call", output_to_operand_aliasing={{0}: (2, {}), {1}: (3, {}), {2}: (4, {})} | custom-call | flops 1000000 | bytes 100000 | tf_op jit(solution)/shard_map/near_attention/pallas_call | solution.py:369
  41.1 0.0 collective-permute-done.11.relayed_values
  41.1 0.0 collective-permute-done.10.relayed_keys
  41.1 2.8 %collective-permute-done.9.far_keys = bf16[272,640]{1,0:T(8,128)(2,1)S(1)} collective-permute-done((bf16[272,640]{1,0:T(8,128)(2,1)S(1)}, bf16[272,640]{1,0:T(8,128)(2,1)S(1)}, u32[]{:S(2)}, u32[]{:S(2)}) %collective-permute-start.9) | collective-permute-done | bytes 348192 | tf_op jit(solution)/shard_map/ppermute | solution.py:444
  43.9 1.1 %far_attention.1 = bf16[512,640]{1,0:T(8,128)(2,1)} custom-call(s32[3]{0:T(128)S(4)} %get-tuple-element.39.info, bf16[512,640]{1,0:T(8,128)(2,1)S(1)} %get-tuple-element.55.query, f32[2,640,256]{2,1,0:T(8,128)S(1)} %get-tuple-element.68.acc_in, f32[2,8,256]{2,1,0:T(8,128)S(1)} %get-tuple-element.69.peak_in, f32[2,8,256]{2,1,0:T(8,128)S(1)} %get-tuple-element.70.mass_in, ...), custom_call_target="tpu_custom_call" | custom-call | flops 1000000 | bytes 100000 | tf_op jit(solution)/shard_map/far_attention/pallas_call | solution.py:412
  (1 shorter events, 0.0 us)
Async XLA Ops:
  11.0 7.9 %collective-permute-start = (bf16[720,256]{1,0:T(8,128)(2,1)S(1)}, bf16[720,256]{1,0:T(8,128)(2,1)S(1)}, u32[]{:S(2)}, u32[]{:S(2)}) collective-permute-start(bf16[720,256]{1,0:T(8,128)(2,1)S(1)} %get-tuple-element.45), channel_id=1, source_target_pairs={{0,4},{4,0},{8,12},{12,8},{16,20},{20,16},{24,28},{28,24},{32,36},... | collective-permute-start | bytes 1105928 | tf_op jit(solution)/shard_map/ppermute | solution.py:441
  11.1 18.9 %collective-permute-start.4 = (bf16[640,512]{1,0:T(8,128)(2,1)S(1)}, bf16[640,512]{1,0:T(8,128)(2,1)S(1)}, u32[]{:S(2)}, u32[]{:S(2)}) collective-permute-start(bf16[640,512]{1,0:T(8,128)(2,1)S(1)} %get-tuple-element.51.value), channel_id=1, source_target_pairs={{0,4},{4,8},{8,12},{12,16},{16,20},{20,24},{24,28},{28,32},{32,36}... | collective-permute-start | bytes 1966088 | tf_op jit(solution)/shard_map/ppermute | solution.py:441
  18.9 5.4 %collective-permute-start.3 = (f32[8,128]{1,0:T(8,128)S(1)}, f32[8,128]{1,0:T(8,128)S(1)}, u32[]{:S(2)}, u32[]{:S(2)}) collective-permute-start(f32[8,128]{1,0:T(8,128)S(1)} %get-tuple-element.47.s0), channel_id=1, source_target_pairs={{0,2},{2,0},{1,3},{3,1},{4,6},{6,4},{5,7},{7,5},{8,10},{10,8},{9,1... | collective-permute-start | bytes 12296 | tf_op jit(solution)/shard_map/ppermute | solution.py:455
  21.1 3.6 %collective-permute-start.2 = (f32[8,128]{1,0:T(8,128)S(1)}, f32[8,128]{1,0:T(8,128)S(1)}, u32[]{:S(2)}, u32[]{:S(2)}) collective-permute-start(f32[8,128]{1,0:T(8,128)S(1)} %get-tuple-element.47.s0), channel_id=1, source_target_pairs={{0,3},{3,0},{1,2},{2,1},{4,7},{7,4},{5,6},{6,5},{8,11},{11,8},{9,1... | collective-permute-start | bytes 12296 | tf_op jit(solution)/shard_map/ppermute | solution.py:455
  21.1 4.2 %collective-permute-start.1 = (f32[8,128]{1,0:T(8,128)S(1)}, f32[8,128]{1,0:T(8,128)S(1)}, u32[]{:S(2)}, u32[]{:S(2)}) collective-permute-start(f32[8,128]{1,0:T(8,128)S(1)} %get-tuple-element.47.s0), channel_id=1, source_target_pairs={{0,1},{1,0},{2,3},{3,2},{4,5},{5,4},{6,7},{7,6},{8,9},{9,8},{10,11... | collective-permute-start | bytes 12296 | tf_op jit(solution)/shard_map/ppermute | solution.py:455
  23.7 12.6 %collective-permute-start.7 = (bf16[720,256]{1,0:T(8,128)(2,1)S(1)}, bf16[720,256]{1,0:T(8,128)(2,1)S(1)}, u32[]{:S(2)}, u32[]{:S(2)}) collective-permute-start(bf16[720,256]{1,0:T(8,128)(2,1)S(1)} %collective-permute-done), channel_id=1, source_target_pairs={{0,4},{4,8},{8,12},{12,16},{16,20},{20,24},{24,28},{28,32},{32,36}... | collective-permute-start | bytes 1105928 | tf_op jit(solution)/shard_map/ppermute | solution.py:441
  25.5 1.9 %collective-permute-start.5 = (bf16[272,640]{1,0:T(8,128)(2,1)S(1)}, bf16[272,640]{1,0:T(8,128)(2,1)S(1)}, u32[]{:S(2)}, u32[]{:S(2)}) collective-permute-start(bf16[272,640]{1,0:T(8,128)(2,1)S(1)} %get-tuple-element.53), channel_id=1, source_target_pairs={{0,4},{4,0},{8,12},{12,8},{16,20},{20,16},{24,28},{28,24},{32,36},... | collective-permute-start | bytes 1044488 | tf_op jit(solution)/shard_map/ppermute | solution.py:441
  25.8 10.5 %collective-permute-start.6 = (bf16[256,640]{1,0:T(8,128)(2,1)S(1)}, bf16[256,640]{1,0:T(8,128)(2,1)S(1)}, u32[]{:S(2)}, u32[]{:S(2)}) collective-permute-start(bf16[256,640]{1,0:T(8,128)(2,1)S(1)} %get-tuple-element.56), channel_id=1, source_target_pairs={{0,4},{4,8},{8,12},{12,16},{16,20},{20,24},{24,28},{28,32},{32,36}... | collective-permute-start | bytes 983048 | tf_op jit(solution)/shard_map/ppermute | solution.py:441
  26.1 14.0 %collective-permute-start.8 = (bf16[288,640]{1,0:T(8,128)(2,1)S(1)}, bf16[288,640]{1,0:T(8,128)(2,1)S(1)}, u32[]{:S(2)}, u32[]{:S(2)}) collective-permute-start(bf16[288,640]{1,0:T(8,128)(2,1)S(1)} %get-tuple-element.67), channel_id=1, source_target_pairs={{0,4},{4,8},{8,12},{12,16},{16,20},{20,24},{24,28},{28,32},{32,36}... | collective-permute-start | bytes 1105928 | tf_op jit(solution)/shard_map/ppermute | solution.py:441
  27.4 16.5 %collective-permute-start.9 = (bf16[272,640]{1,0:T(8,128)(2,1)S(1)}, bf16[272,640]{1,0:T(8,128)(2,1)S(1)}, u32[]{:S(2)}, u32[]{:S(2)}) collective-permute-start(bf16[272,640]{1,0:T(8,128)(2,1)S(1)} %collective-permute-done.5), channel_id=1, source_target_pairs={{0,1},{1,0},{2,3},{3,2},{4,8},{5,9},{6,10},{7,11},{8,4},{9,5},{10,... | collective-permute-start | bytes 1044488 | tf_op jit(solution)/shard_map/ppermute | solution.py:444
  30.0 11.0 %collective-permute-start.11 = (bf16[640,256]{1,0:T(8,128)(2,1)S(1)}, bf16[640,256]{1,0:T(8,128)(2,1)S(1)}, u32[]{:S(2)}, u32[]{:S(2)}) collective-permute-start(bf16[640,256]{1,0:T(8,128)(2,1)S(1)} %later_frame.1), channel_id=1, source_target_pairs={{0,4},{4,0},{8,12},{12,8},{16,20},{20,16},{24,28},{28,24},{32,36},... | collective-permute-start | bytes 983048 | tf_op jit(solution)/shard_map/ppermute | solution.py:441
  36.2 4.9 %collective-permute-start.10 = (bf16[256,640]{1,0:T(8,128)(2,1)S(1)}, bf16[256,640]{1,0:T(8,128)(2,1)S(1)}, u32[]{:S(2)}, u32[]{:S(2)}) collective-permute-start(bf16[256,640]{1,0:T(8,128)(2,1)S(1)} %collective-permute-done.6.keys), channel_id=1, source_target_pairs={{0,4},{4,0},{8,12},{12,8},{16,20},{20,16},{24,28},{28,24},{32,36},... | collective-permute-start | bytes 983048 | tf_op jit(solution)/shard_map/ppermute | solution.py:441

commit v6 on v5

--- a/solution.py
+++ b/solution.py
@@ -11,8 +11,8 @@
 WIN = 4
 EPSILON = 1e-06
 MIB = 2**20
-VALUE_PADDING = 80
-PADDING = 16
+VALUE_PADDING = 48
+PADDING = 8
 EXP2_SCALE = HD ** (-0.5) * 1.4426950408889634
 
 HBM = pl.BlockSpec(memory_space=pltpu.HBM)
@@ -247,13 +247,12 @@
     factor = norm_factor((s0, s1, s2, s3), 0, total_cols)
     half = early.shape[0]
     for c in range(0, key.shape[1], 128):
-        normed = (key[:, c : c + 128] * factor * gain[0:1, c : c + 128]).astype(jnp.bfloat16)
-        all_out[:, c : c + 128] = normed
-        late[:half, c : c + 128] = normed[:half]
-        late[half:, c : c + 128] = normed[: 2 * PADDING]
-        early[:, c : c + 128] = normed[half:]
-        passed[:half, c : c + 128] = normed[half:]
-        passed[half:, c : c + 128] = normed[-PADDING:]
+        cut = slice(c, c + 128)
+        x = key[:, cut] * factor * gain[0:1, cut]
+        all_out[:, cut] = x.astype(jnp.bfloat16)
+        early[:, cut] = x[half:].astype(jnp.bfloat16)
+        late[:, cut] = jnp.concatenate([x[:half], x[: 2 * PADDING]], 0).astype(jnp.bfloat16)
+        passed[:, cut] = jnp.concatenate([x[half:], x[:PADDING]], 0).astype(jnp.bfloat16)
 
 
 def normalise_key(key, gain, sums, total_cols):

time: 45.4 us -> 45.3 us (level)
  Pallas kernels: 23.4 us -> 24.1 us
    pallas_call x1, Pallas kernels: 1.06 us -> 1.79 us  [far_attention(): pl.pallas_call(far_kernel, out_shape=jax.ShapeDtypeStruct((rows, cols), j...]
where the time goes in v6:
time: 45.3 us; the launch traced here: 45.2 us
  Pallas kernels  24.1 us (53%)
  starting transfers between devices  10.5 us (23%)
  waiting for transfers between devices  10.5 us (23%)
    pallas_call x1, Pallas kernels, project_value(): pl.pallas_call(value_kernel, out_shape=(pltpu.VMEM((rows, width), bf16),...  11 us
    pallas_call x1, Pallas kernels, project_query_key(): pl.pallas_call(query_key_kernel, out_shape=(pltpu.VMEM((rows, cols), f32)...  7.3 us
    ppermute x8, waiting for transfers between devices, move(): return lax.ppermute(x, 'queue', pairs)  6.78 us
    ppermute x3, starting transfers between devices, on_device(): lax.ppermute(sums, 'tp', pairs)  4.78 us
    ppermute x8, starting transfers between devices, move(): return lax.ppermute(x, 'queue', pairs)  3.16 us
    ppermute x1, waiting for transfers between devices, move_across(): return lax.ppermute(x, ('queue', 'tp'), across)  2.7 us
    ppermute x1, starting transfers between devices, move_across(): return lax.ppermute(x, ('queue', 'tp'), across)  2.56 us
    pallas_call x1, Pallas kernels, local_attention(): pl.pallas_call(functools.partial(local_kernel, total_cols), out_shape=(pl...  2.15 us
  transfers between devices with their start and end apart: 12, of which 5 were waited for; matrix products, arithmetic and copies ran while one was open for 0% of the time, Pallas kernels for 25%

profile of v6, /device:TPU:66, one launch (start us, length us, event | category | flops | bytes accessed | tf_op | source)
XLA Modules:
  0.0 45.2 jit_solution(2499905634483385318)
XLA Ops:
  0.0 11.0 %project_value.1 = (bf16[512,5120]{1,0:T(8,128)(2,1)S(1)}, bf16[5120,512]{1,0:T(8,128)(2,1)S(1)}, bf16[5120,256]{1,0:T(8,128)(2,1)S(1)}, bf16[640,512]{1,0:T(8,1...) custom-call(s32[2]{0:T(128)} %noise_level.1, ...), custom_call_target="tpu_custom_call" | custom-call | flops 3355443200 | bytes 26000000 | tf_op jit(solution)/shard_map/project_value/pallas_call | solution.py:147
  11.0 0.1 collective-permute-start
  11.1 0.5 %collective-permute-start.4 = (bf16[640,512]{1,0:T(8,128)(2,1)S(1)}, bf16[640,512]{1,0:T(8,128)(2,1)S(1)}, u32[]{:S(2)}, u32[]{:S(2)}) collective-permute-start(bf16[640,512]{1,0:T(8,128)(2,1)S(1)} %get-tuple-element.51.value), channel_id=1, source_target_pairs={{0,4},{4,8},{8,12},{12,16},{16,20},{20,24},{24,28},{28,32},{32,36}... | collective-permute-start | bytes 1966088 | tf_op jit(solution)/shard_map/ppermute | solution.py:440
  11.6 7.3 %project_query_key.1 = (f32[512,640]{1,0:T(8,128)S(1)}, f32[512,640]{1,0:T(8,128)S(1)}, f32[8,128]{1,0:T(8,128)S(1)}) custom-call(bf16[512,5120]{1,0:T(8,128)(2,1)S(1)} %get-tuple-element.40.shaped, bf16[5120,512]{1,0:T(8,128)(2,1)S(1)} %get-tuple-element.41.key_weights, bf16[5120,256]{1,0:T(8,128)(2,1)S(1)} %get-tuple-element.42.mixed_weights, ...), custom_call_target="tpu_custom_call" | custom-call | flops 6710886400 | bytes 18000000 | tf_op jit(solution)/shard_map/project_query_key/pallas_call | solution.py:206
  18.9 0.0 collective-permute-done
  18.9 2.2 %collective-permute-start.3 = (f32[8,128]{1,0:T(8,128)S(1)}, f32[8,128]{1,0:T(8,128)S(1)}, u32[]{:S(2)}, u32[]{:S(2)}) collective-permute-start(f32[8,128]{1,0:T(8,128)S(1)} %get-tuple-element.47.s0), channel_id=1, source_target_pairs={{0,2},{2,0},{1,3},{3,1},{4,6},{6,4},{5,7},{7,5},{8,10},{10,8},{9,1... | collective-permute-start | bytes 12296 | tf_op jit(solution)/shard_map/ppermute | solution.py:454
  21.1 0.0 collective-permute-start.2
  21.1 2.6 %collective-permute-start.1 = (f32[8,128]{1,0:T(8,128)S(1)}, f32[8,128]{1,0:T(8,128)S(1)}, u32[]{:S(2)}, u32[]{:S(2)}) collective-permute-start(f32[8,128]{1,0:T(8,128)S(1)} %get-tuple-element.47.s0), channel_id=1, source_target_pairs={{0,1},{1,0},{2,3},{3,2},{4,5},{5,4},{6,7},{7,6},{8,9},{9,8},{10,11... | collective-permute-start | bytes 12296 | tf_op jit(solution)/shard_map/ppermute | solution.py:454
  23.7 0.6 %collective-permute-start.7 = (bf16[688,256]{1,0:T(8,128)(2,1)S(1)}, bf16[688,256]{1,0:T(8,128)(2,1)S(1)}, u32[]{:S(2)}, u32[]{:S(2)}) collective-permute-start(bf16[688,256]{1,0:T(8,128)(2,1)S(1)} %collective-permute-done), channel_id=1, source_target_pairs={{0,4},{4,8},{8,12},{12,16},{16,20},{20,24},{24,28},{28,32},{32,36}... | collective-permute-start | bytes 1056776 | tf_op jit(solution)/shard_map/ppermute | solution.py:440
  24.3 0.0 collective-permute-done.3.s3
  24.3 0.4 collective-permute-done.2.s2
  24.7 0.6 %collective-permute-done.1.s1 = f32[8,128]{1,0:T(8,128)S(1)} collective-permute-done((f32[8,128]{1,0:T(8,128)S(1)}, f32[8,128]{1,0:T(8,128)S(1)}, u32[]{:S(2)}, u32[]{:S(2)}) %collective-permute-start.1) | collective-permute-done | bytes 4128 | tf_op jit(solution)/shard_map/ppermute | solution.py:454
  25.2 0.3 normalise_key.1
  25.5 0.2 collective-permute-start.5
  25.8 0.4 collective-permute-start.6
  26.1 1.3 %collective-permute-start.8 = (bf16[272,640]{1,0:T(8,128)(2,1)S(1)}, bf16[272,640]{1,0:T(8,128)(2,1)S(1)}, u32[]{:S(2)}, u32[]{:S(2)}) collective-permute-start(bf16[272,640]{1,0:T(8,128)(2,1)S(1)} %get-tuple-element.67), channel_id=1, source_target_pairs={{0,4},{4,8},{8,12},{12,16},{16,20},{20,24},{24,28},{28,32},{32,36}... | collective-permute-start | bytes 1044488 | tf_op jit(solution)/shard_map/ppermute | solution.py:440
  27.4 0.0 collective-permute-done.5
  27.4 2.6 %collective-permute-start.9 = (bf16[264,640]{1,0:T(8,128)(2,1)S(1)}, bf16[264,640]{1,0:T(8,128)(2,1)S(1)}, u32[]{:S(2)}, u32[]{:S(2)}) collective-permute-start(bf16[264,640]{1,0:T(8,128)(2,1)S(1)} %collective-permute-done.5), channel_id=1, source_target_pairs={{0,1},{1,0},{2,3},{3,2},{4,8},{5,9},{6,10},{7,11},{8,4},{9,5},{10,... | collective-permute-start | bytes 1013768 | tf_op jit(solution)/shard_map/ppermute | solution.py:443
  30.0 0.0 collective-permute-done.4.values.value
  30.0 0.1 collective-permute-start.11
  30.1 2.1 %local_attention.1 = (bf16[512,640]{1,0:T(8,128)(2,1)S(1)}, f32[2,640,256]{2,1,0:T(8,128)S(1)}, f32[2,8,256]{2,1,0:T(8,128)S(1)}, f32[2,8,256]{2,1,0:T(8,128)S(1)}) custom-call(s32[3]{0:T(128)S(4)} %get-tuple-element.39.info, f32[512,640]{1,0:T(8,128)S(1)} %get-tuple-element.43.query, f32[1,640]{1,0:T(1,128)S(1)} %get-tuple-element.44.gain, ...), custom_call_target="tpu_custom_call" | custom-call | flops 3000000 | bytes 100000 | tf_op jit(solution)/shard_map/local_attention/pallas_call | solution.py:326
  32.3 3.8 %collective-permute-done.6.keys = bf16[256,640]{1,0:T(8,128)(2,1)S(1)} collective-permute-done((bf16[256,640]{1,0:T(8,128)(2,1)S(1)}, bf16[256,640]{1,0:T(8,128)(2,1)S(1)}, u32[]{:S(2)}, u32[]{:S(2)}) %collective-permute-start.6) | collective-permute-done | bytes 327712 | tf_op jit(solution)/shard_map/ppermute | solution.py:440
  36.0 0.0 collective-permute-done.7.far_values
  36.0 0.0 collective-permute-start.10
  36.0 0.7 %near_attention.2 = (f32[2,640,256]{2,1,0:T(8,128)S(1)}, f32[2,8,256]{2,1,0:T(8,128)S(1)}, f32[2,8,256]{2,1,0:T(8,128)S(1)}) custom-call(s32[3]{0:T(128)S(4)} %get-tuple-element.39.info, bf16[512,640]{1,0:T(8,128)(2,1)S(1)} %get-tuple-element.55.query, ...), custom_call_target="tpu_custom_call", output_to_operand_aliasing={{0}: (2, {}), {1}: (3, {}), {2}: (4, {})} | custom-call | flops 1000000 | bytes 100000 | tf_op jit(solution)/shard_map/near_attention/pallas_call | solution.py:368
  36.8 3.0 %collective-permute-done.8.keys = bf16[272,640]{1,0:T(8,128)(2,1)S(1)} collective-permute-done((bf16[272,640]{1,0:T(8,128)(2,1)S(1)}, bf16[272,640]{1,0:T(8,128)(2,1)S(1)}, u32[]{:S(2)}, u32[]{:S(2)}) %collective-permute-start.8) | collective-permute-done | bytes 348192 | tf_op jit(solution)/shard_map/ppermute | solution.py:440
  39.8 0.9 %near_attention.3 = (f32[2,640,256]{2,1,0:T(8,128)S(1)}, f32[2,8,256]{2,1,0:T(8,128)S(1)}, f32[2,8,256]{2,1,0:T(8,128)S(1)}, bf16[256,640]{1,0:T(8,128)(2,1)S(1)}) custom-call(s32[3]{0:T(128)S(4)} %get-tuple-element.39.info, bf16[512,640]{1,0:T(8,128)(2,1)S(1)} %get-tuple-element.55.query, ...), custom_call_target="tpu_custom_call", output_to_operand_aliasing={{0}: (2, {}), {1}: (3, {}), {2}: (4, {})} | custom-call | flops 1000000 | bytes 100000 | tf_op jit(solution)/shard_map/near_attention/pallas_call | solution.py:368
  40.7 0.0 collective-permute-done.11.relayed_values
  40.7 2.7 %collective-permute-done.9.far_keys = bf16[264,640]{1,0:T(8,128)(2,1)S(1)} collective-permute-done((bf16[264,640]{1,0:T(8,128)(2,1)S(1)}, bf16[264,640]{1,0:T(8,128)(2,1)S(1)}, u32[]{:S(2)}, u32[]{:S(2)}) %collective-permute-start.9) | collective-permute-done | bytes 337952 | tf_op jit(solution)/shard_map/ppermute | solution.py:443
  43.4 0.0 collective-permute-done.10.relayed_keys
  43.4 1.8 %far_attention.1 = bf16[512,640]{1,0:T(8,128)(2,1)} custom-call(s32[3]{0:T(128)S(4)} %get-tuple-element.39.info, bf16[512,640]{1,0:T(8,128)(2,1)S(1)} %get-tuple-element.55.query, f32[2,640,256]{2,1,0:T(8,128)S(1)} %get-tuple-element.68.acc_in, f32[2,8,256]{2,1,0:T(8,128)S(1)} %get-tuple-element.69.peak_in, f32[2,8,256]{2,1,0:T(8,128)S(1)} %get-tuple-element.70.mass_in, ...), custom_call_target="tpu_custom_call" | custom-call | flops 1000000 | bytes 100000 | tf_op jit(solution)/shard_map/far_attention/pallas_call | solution.py:411
  (1 shorter events, 0.0 us)
Async XLA Ops:
  11.0 7.9 %collective-permute-start = (bf16[688,256]{1,0:T(8,128)(2,1)S(1)}, bf16[688,256]{1,0:T(8,128)(2,1)S(1)}, u32[]{:S(2)}, u32[]{:S(2)}) collective-permute-start(bf16[688,256]{1,0:T(8,128)(2,1)S(1)} %get-tuple-element.45), channel_id=1, source_target_pairs={{0,4},{4,0},{8,12},{12,8},{16,20},{20,16},{24,28},{28,24},{32,36},... | collective-permute-start | bytes 1056776 | tf_op jit(solution)/shard_map/ppermute | solution.py:440
  11.1 18.9 %collective-permute-start.4 = (bf16[640,512]{1,0:T(8,128)(2,1)S(1)}, bf16[640,512]{1,0:T(8,128)(2,1)S(1)}, u32[]{:S(2)}, u32[]{:S(2)}) collective-permute-start(bf16[640,512]{1,0:T(8,128)(2,1)S(1)} %get-tuple-element.51.value), channel_id=1, source_target_pairs={{0,4},{4,8},{8,12},{12,16},{16,20},{20,24},{24,28},{28,32},{32,36}... | collective-permute-start | bytes 1966088 | tf_op jit(solution)/shard_map/ppermute | solution.py:440
  18.9 5.4 %collective-permute-start.3 = (f32[8,128]{1,0:T(8,128)S(1)}, f32[8,128]{1,0:T(8,128)S(1)}, u32[]{:S(2)}, u32[]{:S(2)}) collective-permute-start(f32[8,128]{1,0:T(8,128)S(1)} %get-tuple-element.47.s0), channel_id=1, source_target_pairs={{0,2},{2,0},{1,3},{3,1},{4,6},{6,4},{5,7},{7,5},{8,10},{10,8},{9,1... | collective-permute-start | bytes 12296 | tf_op jit(solution)/shard_map/ppermute | solution.py:454
  21.1 3.6 %collective-permute-start.2 = (f32[8,128]{1,0:T(8,128)S(1)}, f32[8,128]{1,0:T(8,128)S(1)}, u32[]{:S(2)}, u32[]{:S(2)}) collective-permute-start(f32[8,128]{1,0:T(8,128)S(1)} %get-tuple-element.47.s0), channel_id=1, source_target_pairs={{0,3},{3,0},{1,2},{2,1},{4,7},{7,4},{5,6},{6,5},{8,11},{11,8},{9,1... | collective-permute-start | bytes 12296 | tf_op jit(solution)/shard_map/ppermute | solution.py:454
  21.1 4.2 %collective-permute-start.1 = (f32[8,128]{1,0:T(8,128)S(1)}, f32[8,128]{1,0:T(8,128)S(1)}, u32[]{:S(2)}, u32[]{:S(2)}) collective-permute-start(f32[8,128]{1,0:T(8,128)S(1)} %get-tuple-element.47.s0), channel_id=1, source_target_pairs={{0,1},{1,0},{2,3},{3,2},{4,5},{5,4},{6,7},{7,6},{8,9},{9,8},{10,11... | collective-permute-start | bytes 12296 | tf_op jit(solution)/shard_map/ppermute | solution.py:454
  23.7 12.4 %collective-permute-start.7 = (bf16[688,256]{1,0:T(8,128)(2,1)S(1)}, bf16[688,256]{1,0:T(8,128)(2,1)S(1)}, u32[]{:S(2)}, u32[]{:S(2)}) collective-permute-start(bf16[688,256]{1,0:T(8,128)(2,1)S(1)} %collective-permute-done), channel_id=1, source_target_pairs={{0,4},{4,8},{8,12},{12,16},{16,20},{20,24},{24,28},{28,32},{32,36}... | collective-permute-start | bytes 1056776 | tf_op jit(solution)/shard_map/ppermute | solution.py:440
  25.5 1.9 %collective-permute-start.5 = (bf16[264,640]{1,0:T(8,128)(2,1)S(1)}, bf16[264,640]{1,0:T(8,128)(2,1)S(1)}, u32[]{:S(2)}, u32[]{:S(2)}) collective-permute-start(bf16[264,640]{1,0:T(8,128)(2,1)S(1)} %get-tuple-element.53), channel_id=1, source_target_pairs={{0,4},{4,0},{8,12},{12,8},{16,20},{20,16},{24,28},{28,24},{32,36},... | collective-permute-start | bytes 1013768 | tf_op jit(solution)/shard_map/ppermute | solution.py:440
  25.8 10.3 %collective-permute-start.6 = (bf16[256,640]{1,0:T(8,128)(2,1)S(1)}, bf16[256,640]{1,0:T(8,128)(2,1)S(1)}, u32[]{:S(2)}, u32[]{:S(2)}) collective-permute-start(bf16[256,640]{1,0:T(8,128)(2,1)S(1)} %get-tuple-element.56), channel_id=1, source_target_pairs={{0,4},{4,8},{8,12},{12,16},{16,20},{20,24},{24,28},{28,32},{32,36}... | collective-permute-start | bytes 983048 | tf_op jit(solution)/shard_map/ppermute | solution.py:440
  26.1 13.6 %collective-permute-start.8 = (bf16[272,640]{1,0:T(8,128)(2,1)S(1)}, bf16[272,640]{1,0:T(8,128)(2,1)S(1)}, u32[]{:S(2)}, u32[]{:S(2)}) collective-permute-start(bf16[272,640]{1,0:T(8,128)(2,1)S(1)} %get-tuple-element.67), channel_id=1, source_target_pairs={{0,4},{4,8},{8,12},{12,16},{16,20},{20,24},{24,28},{28,32},{32,36}... | collective-permute-start | bytes 1044488 | tf_op jit(solution)/shard_map/ppermute | solution.py:440
  27.4 16.0 %collective-permute-start.9 = (bf16[264,640]{1,0:T(8,128)(2,1)S(1)}, bf16[264,640]{1,0:T(8,128)(2,1)S(1)}, u32[]{:S(2)}, u32[]{:S(2)}) collective-permute-start(bf16[264,640]{1,0:T(8,128)(2,1)S(1)} %collective-permute-done.5), channel_id=1, source_target_pairs={{0,1},{1,0},{2,3},{3,2},{4,8},{5,9},{6,10},{7,11},{8,4},{9,5},{10,... | collective-permute-start | bytes 1013768 | tf_op jit(solution)/shard_map/ppermute | solution.py:443
  30.0 10.7 %collective-permute-start.11 = (bf16[640,256]{1,0:T(8,128)(2,1)S(1)}, bf16[640,256]{1,0:T(8,128)(2,1)S(1)}, u32[]{:S(2)}, u32[]{:S(2)}) collective-permute-start(bf16[640,256]{1,0:T(8,128)(2,1)S(1)} %later_frame.1), channel_id=1, source_target_pairs={{0,4},{4,0},{8,12},{12,8},{16,20},{20,16},{24,28},{28,24},{32,36},... | collective-permute-start | bytes 983048 | tf_op jit(solution)/shard_map/ppermute | solution.py:440
  36.0 7.4 %collective-permute-start.10 = (bf16[256,640]{1,0:T(8,128)(2,1)S(1)}, bf16[256,640]{1,0:T(8,128)(2,1)S(1)}, u32[]{:S(2)}, u32[]{:S(2)}) collective-permute-start(bf16[256,640]{1,0:T(8,128)(2,1)S(1)} %collective-permute-done.6.keys), channel_id=1, source_target_pairs={{0,4},{4,0},{8,12},{12,8},{16,20},{20,16},{24,28},{28,24},{32,36},... | collective-permute-start | bytes 983048 | tf_op jit(solution)/shard_map/ppermute | solution.py:440
